TPU v7x, 32 devices: a whole 2x2x4 slice. The times are simulated.
32 devices in a mesh: row: 4 (over y, core), col: 8 (over z, x).
Axes of the slice: x: 2, y: 2, z: 4, core: 2. Of those that a mesh axis runs over, the one named last changes fastest.
Arguments:
- stream_speed: bfloat16 [512, 2048, 32], P('col', 'row'), may hold values from -6 to 6
- normal_speed: bfloat16 [512, 2048, 32], P('col', 'row'), may hold values from -6 to 6
- span_speed: bfloat16 [512, 2048, 32], P('col', 'row'), may hold values from -6 to 6
- stream_first: bfloat16 [2048, 2048], P('row'), may hold values from -0.125 to 0.125
- stream_second: bfloat16 [2048, 2048], P('row'), may hold values from -0.125 to 0.125
- wall_first: bfloat16 [512, 512], replicated, may hold values from -0.25 to 0.25
- wall_second: bfloat16 [512, 512], replicated, may hold values from -0.25 to 0.25
- metric1: float32 [512], replicated, may hold values from 0.5 to 2
- metric2: float32 [512], replicated, may hold values from -1.5 to 1.5
- span_coef: float32 [2, 9], replicated, may hold values from -1 to 1
- counts: int32 [8], replicated, may hold values from 1 to 4, as said below
Outputs:
- tendency: bfloat16 [512, 2048, 32], P('col', 'row')
Inputs may be any that keep to these rules, and one draw needn't show every extreme that they name: counts[b] is the number of fluid planes at the start of spanwise block b of 4 planes; some block is all fluid.
All inputs are finite; a program needn't handle non-finite values.
Results may differ from a plain program's by a relative error of at most 0.0051.
Values may be sent and summed in bfloat16 or wider, within the bound.
No kernel may reach another device: no remote copies, remote signals or barrier semaphores. Data moves between devices by JAX's collectives and lax.ppermute only.
A program may use at most 192 MiB of HBM per device.

v0:
```python
import functools
import math

import jax
import jax.numpy as jnp
from jax import lax
from jax.experimental import pallas as pl
from jax.experimental.pallas import tpu as pltpu
from jax.sharding import PartitionSpec as P

ZB = 4
LANES = 128
ROWS = 16
HALF = 8
CHUNK = 32
VISCOSITY = 0.25
VMEM_BYTES = 63 * 1024 * 1024
NO_COST = pl.CostEstimate(flops=0, bytes_accessed=0, transcendentals=0)


def params(steps):
    return pltpu.CompilerParams(
        dimension_semantics=("arbitrary",) * steps, vmem_limit_bytes=VMEM_BYTES
    )


def unit_lanes(width):
    return LANES if width % LANES == 0 else width


def step_rows(rows):
    return next(g for g in (2 * ROWS, ROWS, rows) if rows % g == 0)


def list_fluid(counts_ref, order_ref):
    planes = order_ref.shape[0]

    def clear(plane, carry):
        order_ref[plane] = 0
        return carry

    lax.fori_loop(0, planes, clear, 0)

    def visit(plane, filled):
        fluid = lax.rem(plane, ZB) < counts_ref[plane // ZB]

        @pl.when(fluid)
        def _():
            order_ref[filled] = plane

        return filled + fluid.astype(jnp.int32)

    return lax.fori_loop(0, planes, visit, 0)


def one_hot_rows(matrix_ref, order, rows, planes, found):
    spread = (2 * rows, rows * planes)
    row = lax.broadcasted_iota(jnp.int32, spread, 0)
    later = row >= rows
    near = lax.broadcasted_iota(jnp.int32, spread, 1) - planes * jnp.where(later, row - rows, row)

    def one(pair, carry):
        slot = 2 * pair
        here = jnp.where(slot < found, order[slot], -rows * planes)
        after = jnp.where(slot + 1 < found, order[slot + 1], -rows * planes)
        hot = jnp.where(near == jnp.where(later, after, here), 1.0, 0.0).astype(jnp.bfloat16)
        start = pl.multiple_of(slot * rows, 2 * rows)
        matrix_ref[pl.ds(start, 2 * rows), :] = hot
        return carry

    lax.fori_loop(0, matrix_ref.shape[0] // (2 * rows), one, 0)


def pack_kernel(counts_ref, spot_ref, u_ref, v_ref, own_ref, pair_ref, *refs):
    *half_refs, order, chosen, rest = refs
    rows, planes, width = u_ref.shape
    kept = own_ref.shape[0]
    parts, apart, _, _, lanes = pair_ref.shape

    @pl.when(pl.program_id(0) == 0)
    def _():
        found = list_fluid(counts_ref, order)
        one_hot_rows(chosen, order, HALF, planes, found)

    def select(ref, first):
        picked = []
        for start in range(0, ROWS, HALF):
            flat = ref[pl.ds(first + start, HALF)].reshape(HALF * planes, width)
            part = jnp.dot(chosen[...], flat, preferred_element_type=jnp.float32)
            picked.append(part.reshape(kept, HALF, width))
        return jnp.concatenate(picked, axis=1).astype(jnp.bfloat16)

    def some(index, carry):
        first = pl.multiple_of(index * ROWS, ROWS)
        here = pl.ds(first, ROWS)
        for field, ref in enumerate((u_ref, v_ref)):
            value = select(ref, first)
            if field == 0:
                own_ref[:, here] = value
            for part in range(parts):
                lane = slice(part * lanes, (part + 1) * lanes)
                pair_ref[part, :, field, here] = value[:apart, :, lane]
            if half_refs:
                rest[...] = value[apart:]
            for mask, half_ref in enumerate(half_refs):
                start = pl.multiple_of((spot_ref[0] ^ mask) * lanes, lanes)
                half_ref[:, field, here] = rest[:, :, pl.ds(start, lanes)]
        return carry

    lax.fori_loop(0, rows // ROWS, some, 0)


def pack(counts, spot, u, v, apart, kept, near):
    rows, planes, width = u.shape
    lanes = unit_lanes(width)
    parts = width // lanes
    group = step_rows(rows)
    others = kept - apart
    halves = near if others > 0 else 0
    return pl.pallas_call(
        pack_kernel,
        grid=(rows // group,),
        out_shape=[
            jax.ShapeDtypeStruct((kept, rows, width), jnp.bfloat16),
            jax.ShapeDtypeStruct((parts, apart, 2, rows, lanes), jnp.bfloat16),
        ]
        + [jax.ShapeDtypeStruct((others, 2, rows, lanes), jnp.bfloat16)] * halves,
        in_specs=[
            pl.BlockSpec(memory_space=pltpu.SMEM),
            pl.BlockSpec(memory_space=pltpu.SMEM),
            pl.BlockSpec((group, planes, width), lambda i: (i, 0, 0)),
            pl.BlockSpec((group, planes, width), lambda i: (i, 0, 0)),
        ],
        out_specs=[
            pl.BlockSpec((kept, group, width), lambda i: (0, i, 0)),
            pl.BlockSpec((parts, apart, 2, group, lanes), lambda i: (0, 0, 0, i, 0)),
        ]
        + [pl.BlockSpec((others, 2, group, lanes), lambda i: (0, 0, i, 0))] * halves,
        scratch_shapes=[
            pltpu.SMEM((planes,), jnp.int32),
            pltpu.VMEM((kept * HALF, HALF * planes), jnp.bfloat16),
            pltpu.VMEM((max(others, 1), ROWS, width), jnp.bfloat16),
        ],
        compiler_params=params(1),
        cost_estimate=NO_COST,
        name="pack",
    )(counts, spot, u, v)


def band_rows(matrix_ref, coef_ref, order, rows, planes):
    taps = coef_ref.shape[1]
    span = rows * planes
    spread = (2 * rows, span)
    row = lax.broadcasted_iota(jnp.int32, spread, 0)
    later = row >= rows
    plane = lax.broadcasted_iota(jnp.int32, spread, 1) - planes * jnp.where(later, row - rows, row)
    inside = (plane >= 0) & (plane < planes)

    def one(pair, carry):
        slot = 2 * pair
        ahead = plane - jnp.where(later, order[slot + 1], order[slot]) + taps // 2
        ahead = jnp.where(ahead < 0, ahead + planes, ahead)
        ahead = jnp.where(ahead >= planes, ahead - planes, ahead)
        ahead = jnp.where(inside, ahead, -1)
        start = pl.multiple_of(slot * rows, 2 * rows)

        def tap(index, values):
            hit = ahead == index
            on_u, on_f = VISCOSITY * coef_ref[1, index], -coef_ref[0, index]
            return (
                values[0] + jnp.where(hit, on_u, 0.0),
                values[1] + jnp.where(hit, on_f, 0.0),
            )

        zero = jnp.zeros(spread, jnp.float32)
        for field, value in enumerate(lax.fori_loop(0, taps, tap, (zero, zero), unroll=True)):
            high = value.astype(jnp.bfloat16)
            low = (value - high.astype(jnp.float32)).astype(jnp.bfloat16)
            matrix_ref[0, pl.ds(start, 2 * rows), field * span : (field + 1) * span] = high
            matrix_ref[1, pl.ds(start, 2 * rows), field * span : (field + 1) * span] = low
        return carry

    lax.fori_loop(0, matrix_ref.shape[1] // (2 * rows), one, 0)


def span_kernel(counts_ref, coef_ref, u_ref, w_ref, out_ref, order, bands):
    rows, planes, width = u_ref.shape
    kept = out_ref.shape[0]

    @pl.when(pl.program_id(0) == 0)
    def _():
        list_fluid(counts_ref, order)
        band_rows(bands, coef_ref, order, HALF, planes)

    def some(index, carry):
        here = pl.ds(pl.multiple_of(index * HALF, HALF), HALF)
        u = u_ref[here].reshape(HALF * planes, width)
        w = w_ref[here].reshape(HALF * planes, width)
        flux = (u.astype(jnp.float32) * w.astype(jnp.float32)).astype(jnp.bfloat16)
        fields = jnp.concatenate([u, flux], axis=0)
        acc = jnp.dot(bands[0], fields, preferred_element_type=jnp.float32)
        acc = acc + jnp.dot(bands[1], fields, preferred_element_type=jnp.float32)
        out_ref[:, here] = acc.reshape(kept, HALF, width)
        return carry

    lax.fori_loop(0, rows // HALF, some, 0)


def span_terms(counts, coef, u, w, kept):
    rows, planes, width = u.shape
    group = step_rows(rows)
    return pl.pallas_call(
        span_kernel,
        grid=(rows // group,),
        out_shape=jax.ShapeDtypeStruct((kept, rows, width), jnp.float32),
        in_specs=[
            pl.BlockSpec(memory_space=pltpu.SMEM),
            pl.BlockSpec(memory_space=pltpu.SMEM),
            pl.BlockSpec((group, planes, width), lambda i: (i, 0, 0)),
            pl.BlockSpec((group, planes, width), lambda i: (i, 0, 0)),
        ],
        out_specs=pl.BlockSpec((kept, group, width), lambda i: (0, i, 0)),
        scratch_shapes=[
            pltpu.SMEM((planes,), jnp.int32),
            pltpu.VMEM((2, kept * HALF, 2 * HALF * planes), jnp.bfloat16),
        ],
        compiler_params=params(1),
        cost_estimate=NO_COST,
        name="span_terms",
    )(counts, coef, u, w)


def stream_kernel(spots_ref, *refs):
    *block_refs, first_ref, second_ref, span_ref, out_ref, matrix, both = refs
    group, rows, width = block_refs[0].shape
    own = first_ref.shape[0]
    places = len(block_refs)

    @pl.when(pl.program_id(0) == 0)
    def _():
        def prepare(place, carry):
            lane = pl.ds(pl.multiple_of(spots_ref[place] * width, width), width)

            def some(index, carry):
                row = pl.ds(pl.multiple_of(index * CHUNK, CHUNK), CHUNK)
                matrix[place, row, :width] = second_ref[row, lane] * jnp.bfloat16(VISCOSITY)
                matrix[place, row, width:] = -first_ref[row, lane]
                return carry

            return lax.fori_loop(0, own // CHUNK, some, carry)

        lax.fori_loop(0, places, prepare, 0)

    for place, ref in enumerate(block_refs):

        def square(slot, carry):
            u = ref[slot]
            full = u.astype(jnp.float32)
            row = pl.ds(pl.multiple_of(slot * rows, rows), rows)
            both[place, row, :width] = u
            both[place, row, width:] = (full * full).astype(jnp.bfloat16)
            return carry

        lax.fori_loop(0, group, square, 0)

    out_ref[...] = span_ref[...]

    def one(place, carry):
        part = lax.dot_general(
            both[place],
            matrix[place],
            (((1,), (1,)), ((), ())),
            preferred_element_type=jnp.float32,
        )
        out_ref[...] += part.reshape(out_ref.shape)
        return carry

    lax.fori_loop(0, places, one, 0)


def stream_terms(spots, blocks, first, second, span):
    kept, rows, width = blocks[0].shape
    own, total = first.shape
    group = min(4, kept)
    by_group = pl.BlockSpec((group, rows, width), lambda i: (i, 0, 0))
    whole = pl.BlockSpec((own, total), lambda i: (0, 0))
    return pl.pallas_call(
        stream_kernel,
        grid=(pl.cdiv(kept, group),),
        out_shape=jax.ShapeDtypeStruct((kept, rows, own), jnp.float32),
        in_specs=[pl.BlockSpec(memory_space=pltpu.SMEM)]
        + [by_group] * len(blocks)
        + [whole, whole, pl.BlockSpec((group, rows, own), lambda i: (i, 0, 0))],
        out_specs=pl.BlockSpec((group, rows, own), lambda i: (i, 0, 0)),
        scratch_shapes=[
            pltpu.VMEM((len(blocks), own, 2 * width), jnp.bfloat16),
            pltpu.VMEM((len(blocks), group * rows, 2 * width), jnp.bfloat16),
        ],
        compiler_params=params(1),
        cost_estimate=NO_COST,
        name="stream_terms",
    )(spots, *blocks, first, second, span)


def swap_rows(array, mask):
    count = lax.axis_size("row")
    return lax.ppermute(array, "row", [(row, row ^ mask) for row in range(count)])


def gather_rows(own, other):
    mask = lax.axis_size("row") // 2
    row = lax.axis_index("row")
    blocks, spots = [own, other], [row, row ^ mask]
    while mask > 1:
        mask //= 2
        blocks = blocks + [swap_rows(block, mask) for block in blocks]
        spots = spots + [spot ^ mask for spot in spots]
    return blocks, jnp.stack(spots).astype(jnp.int32)


def wall_kernel(whole_steps, spot_ref, matrix_ref, pair_ref, *refs):
    *half_refs, out_ref, lines = refs
    sources, group, _, rows, lanes = pair_ref.shape
    total = sources * rows
    step = pl.program_id(0)
    pack_units = 2 if group % 2 == 0 else 1

    def both(u, v):
        return u, (u.astype(jnp.float32) * v.astype(jnp.float32)).astype(jnp.bfloat16)

    def put(unit, terms):
        terms = terms.astype(jnp.bfloat16)
        for k in range(pack_units):
            lane = slice(k * lanes, (k + 1) * lanes)
            out_ref[:, unit + k] = terms[:, lane].reshape(sources, rows, lanes)

    @pl.when(step < whole_steps)
    def _():
        def some(index, carry):
            unit = index * pack_units
            for k in range(pack_units):
                u, flux = both(pair_ref[:, unit + k, 0], pair_ref[:, unit + k, 1])
                lane = slice(k * lanes, (k + 1) * lanes)
                lines[:total, lane] = u.reshape(total, lanes)
                lines[total:, lane] = flux.reshape(total, lanes)
            put(unit, jnp.dot(matrix_ref[...], lines[...], preferred_element_type=jnp.float32))
            return carry

        lax.fori_loop(0, group // pack_units, some, 0)

    if len(half_refs) == 0:
        return
    near = total // 2

    @pl.when(step >= whole_steps)
    def _():
        def some(index, carry):
            unit = index * pack_units
            for mask, ref in enumerate(half_refs):
                start = pl.multiple_of((spot_ref[0] ^ mask) * rows, rows)
                for k in range(pack_units):
                    u, flux = both(ref[unit + k, 0], ref[unit + k, 1])
                    lane = slice(k * lanes, (k + 1) * lanes)
                    lines[pl.ds(start, rows), lane] = u
                    lines[pl.ds(start + near, rows), lane] = flux
            on_u = pl.ds(pl.multiple_of(spot_ref[1] * near, near), near)
            on_flux = pl.ds(pl.multiple_of(total + spot_ref[1] * near, near), near)
            terms = jnp.dot(
                matrix_ref[:, on_u], lines[:near], preferred_element_type=jnp.float32
            ) + jnp.dot(
                matrix_ref[:, on_flux], lines[near : 2 * near], preferred_element_type=jnp.float32
            )
            put(unit, terms)
            return carry

        lax.fori_loop(0, group // pack_units, some, 0)


def wall_terms(spot, matrix, pairs, halves):
    sources, units, _, rows, lanes = pairs.shape
    more = halves[0].shape[0] if halves else 0
    group = next(g for g in (4, 6, 10, 2, 1) if units % g == 0)
    whole_steps = units // group
    pack_units = 2 if group % 2 == 0 else 1
    half_blocks = [
        pl.BlockSpec((group, 2, rows, lanes), lambda i: (jnp.maximum(i - whole_steps, 0), 0, 0, 0))
    ] * len(halves)
    return pl.pallas_call(
        functools.partial(wall_kernel, whole_steps),
        grid=(whole_steps + pl.cdiv(more, group),),
        out_shape=jax.ShapeDtypeStruct((sources, units + more, rows, lanes), jnp.bfloat16),
        in_specs=[
            pl.BlockSpec(memory_space=pltpu.SMEM),
            pl.BlockSpec(matrix.shape, lambda i: (0, 0)),
            pl.BlockSpec(
                (sources, group, 2, rows, lanes),
                lambda i: (0, jnp.minimum(i, whole_steps - 1), 0, 0, 0),
            ),
        ]
        + half_blocks,
        out_specs=pl.BlockSpec((sources, group, rows, lanes), lambda i: (0, i, 0, 0)),
        scratch_shapes=[pltpu.VMEM((2 * sources * rows, pack_units * lanes), jnp.bfloat16)],
        compiler_params=params(1),
        cost_estimate=NO_COST,
        name="wall_terms",
    )(spot, matrix, pairs, *halves)


def finish_kernel(apart, counts_ref, base_ref, wall_ref, out_ref, order, chosen, placed):
    rows, planes, width = out_ref.shape
    kept = base_ref.shape[0]
    places, units, _, lanes = wall_ref.shape
    parts = width // lanes
    whole = parts * apart // places

    @pl.when(pl.program_id(0) == 0)
    def _():
        found = list_fluid(counts_ref, order)
        one_hot_rows(chosen, order, HALF, planes, found)
        placed[...] = chosen[...].T

    def some(index, carry):
        here = pl.ds(pl.multiple_of(index * ROWS, ROWS), ROWS)
        columns = []
        for part in range(parts):
            first = part * places // parts
            pieces = [wall_ref[first + k, :whole, here] for k in range(places // parts)]
            column = jnp.concatenate(pieces, axis=0).astype(jnp.float32)
            if units > whole:
                low = wall_ref[part, whole:, here].astype(jnp.float32)
                high = wall_ref[part + parts, whole:, here].astype(jnp.float32)
                column = jnp.concatenate([column, low + high], axis=0)
            columns.append(column)
        value = base_ref[:, here] + jnp.concatenate(columns, axis=-1)
        for start in range(0, ROWS, HALF):
            some_rows = value[:, start : start + HALF].reshape(kept * HALF, width)
            out = jnp.dot(
                placed[...], some_rows.astype(jnp.bfloat16), preferred_element_type=jnp.float32
            )
            out_ref[pl.ds(index * ROWS + start, HALF)] = out.astype(jnp.bfloat16).reshape(
                HALF, planes, width
            )
        return carry

    lax.fori_loop(0, rows // ROWS, some, 0)


def finish(counts, base, wall, planes, apart):
    kept, rows, width = base.shape
    places, units, _, lanes = wall.shape
    group = step_rows(rows)
    return pl.pallas_call(
        functools.partial(finish_kernel, apart),
        grid=(rows // group,),
        out_shape=jax.ShapeDtypeStruct((rows, planes, width), jnp.bfloat16),
        in_specs=[
            pl.BlockSpec(memory_space=pltpu.SMEM),
            pl.BlockSpec((kept, group, width), lambda i: (0, i, 0)),
            pl.BlockSpec((places, units, group, lanes), lambda i: (0, 0, i, 0)),
        ],
        out_specs=pl.BlockSpec((group, planes, width), lambda i: (i, 0, 0)),
        scratch_shapes=[
            pltpu.SMEM((planes,), jnp.int32),
            pltpu.VMEM((kept * HALF, HALF * planes), jnp.bfloat16),
            pltpu.VMEM((HALF * planes, kept * HALF), jnp.bfloat16),
        ],
        compiler_params=params(1),
        cost_estimate=NO_COST,
        name="finish",
    )(counts, base, wall)


def swap(array, mask):
    count = lax.axis_size("col")
    if mask == 0:
        return array
    return lax.ppermute(array, "col", [(column, column ^ mask) for column in range(count)])


def with_kept(
    apart, kept, u, v, w, first, second, wall_first, wall_second, metric1, metric2, coef, counts
):
    rows, planes, width = u.shape
    columns = lax.axis_size("col")
    column = lax.axis_index("col")
    near = columns // 2
    spot = jnp.stack([column % near, column // near]).astype(jnp.int32)
    own, pairs, *halves = pack(counts, spot, u, v, apart, kept, near)
    parts, _, _, _, lanes = pairs.shape
    units = parts * apart // columns
    lines = lax.all_to_all(
        pairs.reshape(columns, units, 2, rows, lanes), "col", split_axis=0, concat_axis=0
    )
    halves = [swap(half, mask) for mask, half in enumerate(halves)]
    one, two = metric1[:, None], metric2[:, None]
    wide_first = wall_first.astype(jnp.float32)
    on_stream = VISCOSITY * (one * one * wall_second.astype(jnp.float32) + two * wide_first)
    matrix = jnp.concatenate([on_stream, -one * wide_first], axis=1).astype(jnp.bfloat16)
    first_block = swap_rows(own, lax.axis_size("row") // 2)
    lines, halves, first_block = lax.optimization_barrier((lines, halves, first_block))
    wall = wall_terms(spot, matrix, lines, halves)
    wall = lax.all_to_all(wall, "col", split_axis=0, concat_axis=0)
    blocks, spots = gather_rows(own, first_block)
    span = span_terms(counts, coef, u, w, kept)
    base = stream_terms(spots, blocks, first, second, span)
    return finish(counts, base, wall, planes, apart)


def share_of(kept, parts, columns):
    if 2 * parts != columns:
        return kept
    options = range(columns // 2, kept + 1, columns // 2)
    return min(options, key=lambda a: max(2 * a, 1.5 * a + kept - a) + a + 2 * (kept - a))


def on_device(u, v, w, first, second, wall_first, wall_second, metric1, metric2, coef, counts):
    u, v, w = (jnp.swapaxes(t, 1, 2) for t in (u, v, w))
    planes, width = u.shape[1:]
    columns = lax.axis_size("col")
    parts = width // unit_lanes(width)
    step = 2 if 2 * parts == columns else columns // math.gcd(columns, parts)
    blocks = counts.shape[0]
    least, middle = blocks - 1 + ZB, (blocks - 1) * (ZB + 1) / 2 + ZB
    sizes = [size for size in range(step, planes, step) if size >= least]
    sizes = [size for size in sizes if abs(size - middle) < 3.5 * step] + [planes]
    branches = [
        functools.partial(with_kept, share_of(size, parts, columns), size) for size in sizes
    ]
    fluid = jnp.sum(counts)
    index = (fluid - sizes[0] + (step - 1)) // step
    operands = (u, v, w, first, second, wall_first, wall_second, metric1, metric2, coef, counts)
    out = lax.switch(index, branches, *operands)
    return jnp.swapaxes(out, 1, 2)


def solution(mesh):
    field = P("col", "row", None)
    placed = (field, field, field, P("row", None), P("row", None)) + (P(),) * 6
    return jax.shard_map(
        on_device,
        mesh=mesh,
        in_specs=placed,
        out_specs=field,
        check_vma=False,
    )
```

profile of v0, /device:TPU:0, one launch (start us, length us, event | category | flops | bytes accessed | tf_op | source)
XLA Modules:
  0.0 128.1 jit_solution(11664625390067559098)
XLA Ops:
  0.0 1.3 %reduce_sum.9 = s32[]{:T(128)} reduce(s32[8]{0:T(128)} %param.29, s32[]{:T(128)} %constant.291.clone.1), dimensions={0}, to_apply=%region_0.0 | reduce | flops 7 | bytes 40 | tf_op jit(solution)/shard_map/reduce_sum | solution.py:529
  2.0 126.1 %conditional.1 = (bf16[64,32,512]{2,1,0:T(8,128)(2,1)}) conditional(s32[]{:T(128)} %clamp.3, (s32[8]{0:T(128)}, bf16[64,32,512]{2,1,0:T(8,128)(2,1)}, bf16[64,32,512]{2,1,0:T(8,128)(2,1)}, f32[2,9]{1,0:T(2,128)}, bf16[64,32,512]{2,1,0:T(8,128)(2,1)}, /*index=5*/bf16[512,2048]{1,0:T(8,128)(2,1)}, ...), branch_computations={%region_1.2_spmd, %region_2.3_spmd, %region_3.4_spmd, %region_4.5_... | conditional | flops 4457513 | bytes 59536664 | solution.py:532
  2.2 0.6 pad_add_fusion.9.spot_ref
  2.8 5.5 %pack.12 = (bf16[24,64,512]{2,1,0:T(8,128)(2,1)}, bf16[4,16,2,64,128]{4,3,2,1,0:T(8,128)(2,1)}, bf16[8,2,64,128]{3,2,1,0:T(8,128)(2,1)}, bf16[8,2,64,128]{3,2,1,...) custom-call(s32[8]{0:T(128)} %get-tuple-element.282.counts_ref, ...), custom_call_target="tpu_custom_call" | custom-call | tf_op jit(solution)/shard_map/cond/branch_4_fun/pack/pallas_call | solution.py:120
  8.3 0.0 copy-start.45
  8.4 0.0 copy-start.4
  8.4 0.0 copy-start.12
  8.4 0.0 copy-start.37
  8.4 7.4 %all-to-all-start.8 = ((bf16[8,8,2,64,128]{4,3,2,1,0:T(8,128)(2,1)}), bf16[8,8,2,64,128]{4,3,2,1,0:T(8,128)(2,1)}, u32[]{:S(2)}, u32[]{:S(2)}) async-start(bf16[8,8,2,64,128]{4,3,2,1,0:T(8,128)(2,1)} %bitcast.85), calls=%async_computation.8 | async-start | bytes 4194304 | tf_op jit(solution)/shard_map/cond/branch_4_fun/all_to_all | solution.py:491
  15.8 1.5 %collective-permute-start.27 = (bf16[24,64,512]{2,1,0:T(8,128)(2,1)}, bf16[24,64,512]{2,1,0:T(8,128)(2,1)}, u32[]{:S(2)}, u32[]{:S(2)}) collective-permute-start(bf16[24,64,512]{2,1,0:T(8,128)(2,1)} %get-tuple-element.285.refs_0_), channel_id=1, source_target_pairs={{0,16},{8,24},{16,0},{24,8},{1,17},{9,25},{17,1},{25,9},{2,18},{10... | collective-permute-start | bytes 4718600 | tf_op jit(solution)/shard_map/cond/branch_4_fun/ppermute | solution.py:307
  17.3 2.0 %collective-permute-start.24 = (bf16[8,2,64,128]{3,2,1,0:T(8,128)(2,1)S(1)}, bf16[8,2,64,128]{3,2,1,0:T(8,128)(2,1)S(1)}, u32[]{:S(2)}, u32[]{:S(2)}) collective-permute-start(bf16[8,2,64,128]{3,2,1,0:T(8,128)(2,1)S(1)} %copy-done.75), channel_id=1, source_target_pairs={{0,1},{1,0},{2,3},{3,2},{4,5},{5,4},{6,7},{7,6},{8,9},{9,8},{10,11... | collective-permute-start | bytes 786440 | tf_op jit(solution)/shard_map/cond/branch_4_fun/ppermute | solution.py:477
  19.3 1.5 %collective-permute-start.25 = (bf16[8,2,64,128]{3,2,1,0:T(8,128)(2,1)S(1)}, bf16[8,2,64,128]{3,2,1,0:T(8,128)(2,1)}, u32[]{:S(2)}, u32[]{:S(2)}) collective-permute-start(bf16[8,2,64,128]{3,2,1,0:T(8,128)(2,1)S(1)} %copy-done.72), channel_id=1, source_target_pairs={{0,2},{1,3},{2,0},{3,1},{4,6},{5,7},{6,4},{7,5},{8,10},{9,11},{10,... | collective-permute-start | bytes 786440 | tf_op jit(solution)/shard_map/cond/branch_4_fun/ppermute | solution.py:477
  20.8 0.1 collective-permute-start.26
  20.9 0.0 copy-done.45
  20.9 0.4 fusion.18
  21.3 1.2 pad_maximum_fusion.4.matrix_ref
  22.4 17.2 %collective-permute-done.24.refs_1_ = bf16[8,2,64,128]{3,2,1,0:T(8,128)(2,1)S(1)} collective-permute-done((bf16[8,2,64,128]{3,2,1,0:T(8,128)(2,1)S(1)}, bf16[8,2,64,128]{3,2,1,0:T(8,128)(2,1)S(1)}, u32[]{:S(2)}, u32[]{:S(2)}) %collective-permute-start.24) | collective-permute-done | bytes 262176 | tf_op jit(solution)/shard_map/cond/branch_4_fun/ppermute | solution.py:477
  39.7 17.9 %collective-permute-done.25.refs_2_ = bf16[8,2,64,128]{3,2,1,0:T(8,128)(2,1)} collective-permute-done((bf16[8,2,64,128]{3,2,1,0:T(8,128)(2,1)S(1)}, bf16[8,2,64,128]{3,2,1,0:T(8,128)(2,1)}, u32[]{:S(2)}, u32[]{:S(2)}) %collective-permute-start.25) | collective-permute-done | bytes 262176 | tf_op jit(solution)/shard_map/cond/branch_4_fun/ppermute | solution.py:477
  57.5 4.4 %collective-permute-done.26.refs_3_ = bf16[8,2,64,128]{3,2,1,0:T(8,128)(2,1)} collective-permute-done((bf16[8,2,64,128]{3,2,1,0:T(8,128)(2,1)S(1)}, bf16[8,2,64,128]{3,2,1,0:T(8,128)(2,1)}, u32[]{:S(2)}, u32[]{:S(2)}) %collective-permute-start.26) | collective-permute-done | bytes 262176 | tf_op jit(solution)/shard_map/cond/branch_4_fun/ppermute | solution.py:477
  62.0 0.0 collective-permute-done.27.refs_1_
  62.0 2.2 %all-to-all-done.8.pair_ref = bf16[8,8,2,64,128]{4,3,2,1,0:T(8,128)(2,1)} async-done(((bf16[8,8,2,64,128]{4,3,2,1,0:T(8,128)(2,1)}), bf16[8,8,2,64,128]{4,3,2,1,0:T(8,128)(2,1)}, u32[]{:S(2)}, u32[]{:S(2)}) %all-to-all-start.8) | async-done | bytes 2097184 | tf_op jit(solution)/shard_map/cond/branch_4_fun/all_to_all | solution.py:491
  64.1 6.6 %wall_terms.12 = bf16[8,16,64,128]{3,2,1,0:T(8,128)(2,1)} custom-call(s32[2]{0:T(128)} %pad_add_fusion.9.spot_ref, bf16[512,1024]{1,0:T(8,128)(2,1)} %pad_maximum_fusion.4.matrix_ref, bf16[8,8,2,64,128]{4,3,2,1,0:T(8,128)(2,1)} %all-to-all-done.8.pair_ref, bf16[8,2,64,128]{3,2,1,0:T(8,128)(2,1)} %get-tuple-element.301.refs_0_, ...), custom_call_target="tpu_custom_call" | custom-call | tf_op jit(solution)/shard_map/cond/branch_4_fun/wall_terms/pallas_call | solution.py:388
  70.7 4.5 %all-to-all-start.9 = ((bf16[8,16,64,128]{3,2,1,0:T(8,128)(2,1)}), bf16[8,16,64,128]{3,2,1,0:T(8,128)(2,1)}, u32[]{:S(2)}, u32[]{:S(2)}) async-start(bf16[8,16,64,128]{3,2,1,0:T(8,128)(2,1)} %wall_terms.12), calls=%async_computation.9 | async-start | bytes 4194304 | tf_op jit(solution)/shard_map/cond/branch_4_fun/all_to_all | solution.py:502
  75.2 0.1 collective-permute-start.28
  75.3 0.5 collective-permute-start.29
  75.8 7.1 %span_terms.12.refs_6_ = f32[24,64,512]{2,1,0:T(8,128)} custom-call(s32[8]{0:T(128)S(1)} %copy-done.24, f32[2,9]{1,0:T(2,128)S(1)} %copy-done.53, bf16[64,32,512]{2,1,0:T(8,128)(2,1)} %get-tuple-element.283.u_ref, bf16[64,32,512]{2,1,0:T(8,128)(2,1)} %get-tuple-element.295.w_ref), custom_call_target="tpu_custom_call" | custom-call | tf_op jit(solution)/shard_map/cond/branch_4_fun/span_terms/pallas_call | solution.py:212
  82.9 0.7 pad_add_fusion.8.spots_ref
  83.6 0.0 collective-permute-done.28.refs_2_
  83.6 0.0 collective-permute-done.29.refs_3_
  83.6 17.7 %stream_terms.12.base_ref = f32[24,64,512]{2,1,0:T(8,128)} custom-call(s32[4]{0:T(128)} %pad_add_fusion.8.spots_ref, bf16[24,64,512]{2,1,0:T(8,128)(2,1)} %get-tuple-element.285.refs_0_, bf16[24,64,512]{2,1,0:T(8,128)(2,1)} %collective-permute-done.27.refs_1_, bf16[24,64,512]{2,1,0:T(8,128)(2,1)} %collective-permute-done.28.refs_2_, ...), custom_call_target="tpu_custom_call" | custom-call | tf_op jit(solution)/shard_map/cond/branch_4_fun/stream_terms/pallas_call | solution.py:287
  101.3 21.8 %all-to-all-done.9.wall_ref = bf16[8,16,64,128]{3,2,1,0:T(8,128)(2,1)} async-done(((bf16[8,16,64,128]{3,2,1,0:T(8,128)(2,1)}), bf16[8,16,64,128]{3,2,1,0:T(8,128)(2,1)}, u32[]{:S(2)}, u32[]{:S(2)}) %all-to-all-start.9) | async-done | bytes 2097184 | tf_op jit(solution)/shard_map/cond/branch_4_fun/all_to_all | solution.py:502
  123.1 5.0 %finish.12 = bf16[64,32,512]{2,1,0:T(8,128)(2,1)} custom-call(s32[8]{0:T(128)S(1)} %copy-done.24, f32[24,64,512]{2,1,0:T(8,128)} %stream_terms.12.base_ref, bf16[8,16,64,128]{3,2,1,0:T(8,128)(2,1)} %all-to-all-done.9.wall_ref), custom_call_target="tpu_custom_call" | custom-call | tf_op jit(solution)/shard_map/cond/branch_4_fun/finish/pallas_call | solution.py:452
  (16 shorter events, 0.0 us)
Async XLA Ops:
  8.3 9.0 %copy-start.75 = (bf16[8,2,64,128]{3,2,1,0:T(8,128)(2,1)S(1)}, bf16[8,2,64,128]{3,2,1,0:T(8,128)(2,1)}, u32[]{:S(2)}) copy-start(bf16[8,2,64,128]{3,2,1,0:T(8,128)(2,1)} %get-tuple-element.288) | copy-start | bytes 786436 | tf_op jit(solution)/shard_map/cond
  8.3 11.0 %copy-start.72 = (bf16[8,2,64,128]{3,2,1,0:T(8,128)(2,1)S(1)}, bf16[8,2,64,128]{3,2,1,0:T(8,128)(2,1)}, u32[]{:S(2)}) copy-start(bf16[8,2,64,128]{3,2,1,0:T(8,128)(2,1)} %get-tuple-element.289) | copy-start | bytes 786436 | tf_op jit(solution)/shard_map/cond
  8.3 12.5 %copy-start.69 = (bf16[8,2,64,128]{3,2,1,0:T(8,128)(2,1)S(1)}, bf16[8,2,64,128]{3,2,1,0:T(8,128)(2,1)}, u32[]{:S(2)}) copy-start(bf16[8,2,64,128]{3,2,1,0:T(8,128)(2,1)} %get-tuple-element.290) | copy-start | bytes 786436 | tf_op jit(solution)/shard_map/cond
  8.3 12.5 %copy-start.45 = (f32[512]{0:T(512)S(1)}, f32[512]{0:T(512)}, u32[]{:S(2)}) copy-start(f32[512]{0:T(512)} %get-tuple-element.296) | copy-start | bytes 6148 | tf_op jit(solution)/shard_map/cond
  8.4 12.5 %copy-start.4 = (bf16[512,512]{1,0:T(8,128)(2,1)S(1)}, bf16[512,512]{1,0:T(8,128)(2,1)}, u32[]{:S(2)}) copy-start(bf16[512,512]{1,0:T(8,128)(2,1)} %get-tuple-element.297) | copy-start | bytes 1572868 | tf_op jit(solution)/shard_map/cond
  8.4 12.5 %copy-start.12 = (bf16[512,512]{1,0:T(8,128)(2,1)S(1)}, bf16[512,512]{1,0:T(8,128)(2,1)}, u32[]{:S(2)}) copy-start(bf16[512,512]{1,0:T(8,128)(2,1)} %get-tuple-element.299) | copy-start | bytes 1572868 | tf_op jit(solution)/shard_map/cond
  8.4 12.5 %copy-start.37 = (f32[512]{0:T(512)S(1)}, f32[512]{0:T(512)}, u32[]{:S(2)}) copy-start(f32[512]{0:T(512)} %get-tuple-element.298) | copy-start | bytes 6148 | tf_op jit(solution)/shard_map/cond
  8.4 55.7 %all-to-all-start.8 = ((bf16[8,8,2,64,128]{4,3,2,1,0:T(8,128)(2,1)}), bf16[8,8,2,64,128]{4,3,2,1,0:T(8,128)(2,1)}, u32[]{:S(2)}, u32[]{:S(2)}) async-start(bf16[8,8,2,64,128]{4,3,2,1,0:T(8,128)(2,1)} %bitcast.85), calls=%async_computation.8 | async-start | bytes 4194304 | tf_op jit(solution)/shard_map/cond/branch_4_fun/all_to_all | solution.py:491
  15.8 46.2 %collective-permute-start.27 = (bf16[24,64,512]{2,1,0:T(8,128)(2,1)}, bf16[24,64,512]{2,1,0:T(8,128)(2,1)}, u32[]{:S(2)}, u32[]{:S(2)}) collective-permute-start(bf16[24,64,512]{2,1,0:T(8,128)(2,1)} %get-tuple-element.285.refs_0_), channel_id=1, source_target_pairs={{0,16},{8,24},{16,0},{24,8},{1,17},{9,25},{17,1},{25,9},{2,18},{10... | collective-permute-start | bytes 4718600 | tf_op jit(solution)/shard_map/cond/branch_4_fun/ppermute | solution.py:307
  17.3 22.4 %collective-permute-start.24 = (bf16[8,2,64,128]{3,2,1,0:T(8,128)(2,1)S(1)}, bf16[8,2,64,128]{3,2,1,0:T(8,128)(2,1)S(1)}, u32[]{:S(2)}, u32[]{:S(2)}) collective-permute-start(bf16[8,2,64,128]{3,2,1,0:T(8,128)(2,1)S(1)} %copy-done.75), channel_id=1, source_target_pairs={{0,1},{1,0},{2,3},{3,2},{4,5},{5,4},{6,7},{7,6},{8,9},{9,8},{10,11... | collective-permute-start | bytes 786440 | tf_op jit(solution)/shard_map/cond/branch_4_fun/ppermute | solution.py:477
  19.3 38.2 %collective-permute-start.25 = (bf16[8,2,64,128]{3,2,1,0:T(8,128)(2,1)S(1)}, bf16[8,2,64,128]{3,2,1,0:T(8,128)(2,1)}, u32[]{:S(2)}, u32[]{:S(2)}) collective-permute-start(bf16[8,2,64,128]{3,2,1,0:T(8,128)(2,1)S(1)} %copy-done.72), channel_id=1, source_target_pairs={{0,2},{1,3},{2,0},{3,1},{4,6},{5,7},{6,4},{7,5},{8,10},{9,11},{10,... | collective-permute-start | bytes 786440 | tf_op jit(solution)/shard_map/cond/branch_4_fun/ppermute | solution.py:477
  20.8 41.2 %collective-permute-start.26 = (bf16[8,2,64,128]{3,2,1,0:T(8,128)(2,1)S(1)}, bf16[8,2,64,128]{3,2,1,0:T(8,128)(2,1)}, u32[]{:S(2)}, u32[]{:S(2)}) collective-permute-start(bf16[8,2,64,128]{3,2,1,0:T(8,128)(2,1)S(1)} %copy-done.69), channel_id=1, source_target_pairs={{0,3},{1,2},{2,1},{3,0},{4,7},{5,6},{6,5},{7,4},{8,11},{9,10},{10,... | collective-permute-start | bytes 786440 | tf_op jit(solution)/shard_map/cond/branch_4_fun/ppermute | solution.py:477
  39.7 24.5 %copy-start.30 = (bf16[8,2,64,128]{3,2,1,0:T(8,128)(2,1)}, bf16[8,2,64,128]{3,2,1,0:T(8,128)(2,1)S(1)}, u32[]{:S(2)}) copy-start(bf16[8,2,64,128]{3,2,1,0:T(8,128)(2,1)S(1)} %collective-permute-done.24.refs_1_) | copy-start | bytes 786436 | tf_op jit(solution)/shard_map/cond
  70.7 5.1 %copy-start.24 = (s32[8]{0:T(128)S(1)}, s32[8]{0:T(128)}, u32[]{:S(2)}) copy-start(s32[8]{0:T(128)} %get-tuple-element.282.counts_ref) | copy-start | bytes 100 | tf_op jit(solution)/shard_map/cond
  70.7 5.1 %copy-start.53 = (f32[2,9]{1,0:T(2,128)S(1)}, f32[2,9]{1,0:T(2,128)}, u32[]{:S(2)}) copy-start(f32[2,9]{1,0:T(2,128)} %get-tuple-element.294.coef_ref) | copy-start | bytes 220 | tf_op jit(solution)/shard_map/cond
  70.7 52.4 %all-to-all-start.9 = ((bf16[8,16,64,128]{3,2,1,0:T(8,128)(2,1)}), bf16[8,16,64,128]{3,2,1,0:T(8,128)(2,1)}, u32[]{:S(2)}, u32[]{:S(2)}) async-start(bf16[8,16,64,128]{3,2,1,0:T(8,128)(2,1)} %wall_terms.12), calls=%async_computation.9 | async-start | bytes 4194304 | tf_op jit(solution)/shard_map/cond/branch_4_fun/all_to_all | solution.py:502
  75.2 8.4 %collective-permute-start.28 = (bf16[24,64,512]{2,1,0:T(8,128)(2,1)}, bf16[24,64,512]{2,1,0:T(8,128)(2,1)}, u32[]{:S(2)}, u32[]{:S(2)}) collective-permute-start(bf16[24,64,512]{2,1,0:T(8,128)(2,1)} %get-tuple-element.285.refs_0_), channel_id=1, source_target_pairs={{0,8},{8,0},{16,24},{24,16},{1,9},{9,1},{17,25},{25,17},{2,10},{10... | collective-permute-start | bytes 4718600 | tf_op jit(solution)/shard_map/cond/branch_4_fun/ppermute | solution.py:307
  75.3 8.3 %collective-permute-start.29 = (bf16[24,64,512]{2,1,0:T(8,128)(2,1)}, bf16[24,64,512]{2,1,0:T(8,128)(2,1)}, u32[]{:S(2)}, u32[]{:S(2)}) collective-permute-start(bf16[24,64,512]{2,1,0:T(8,128)(2,1)} %collective-permute-done.27.refs_1_), channel_id=1, source_target_pairs={{0,8},{8,0},{16,24},{24,16},{1,9},{9,1},{17,25},{25,17},{2,10},{10... | collective-permute-start | bytes 4718600 | tf_op jit(solution)/shard_map/cond/branch_4_fun/ppermute | solution.py:307
where the time goes:
time: 128 us
  waiting for transfers between devices  63.5 us (50%)
  Pallas kernels  41.9 us (33%)
  starting transfers between devices  17.6 us (14%)
  other arithmetic  4.07 us (3%)
    ppermute x3, waiting for transfers between devices, swap(): lax.ppermute(array, 'col', [(column, column ^ mask) for column in range(c...  39.5 us
    all_to_all x1, waiting for transfers between devices, with_kept(): wall = lax.all_to_all(wall, 'col', split_axis=0, concat_axis=0)  21.8 us
    pallas_call x1, Pallas kernels, stream_terms(): pl.pallas_call(stream_kernel, grid=(pl.cdiv(kept, group),), out_shape=jax...  17.7 us
    all_to_all x1, starting transfers between devices, with_kept(): lax.all_to_all(pairs.reshape(columns, units, 2, rows, lanes), 'col', spli...  7.42 us
    pallas_call x1, Pallas kernels, span_terms(): pl.pallas_call(span_kernel, grid=(rows // group,), out_shape=jax.ShapeDty...  7.12 us
    pallas_call x1, Pallas kernels, wall_terms(): pl.pallas_call(functools.partial(wall_kernel, whole_steps), grid=(whole_s...  6.56 us
    pallas_call x1, Pallas kernels, pack(): pl.pallas_call(pack_kernel, grid=(rows // group,), out_shape=[jax.ShapeDt...  5.48 us
    pallas_call x1, Pallas kernels, finish(): pl.pallas_call(functools.partial(finish_kernel, apart), grid=(rows // gro...  4.99 us
  transfers between devices with their start and end apart: 8, of which 5 were waited for; matrix products, arithmetic and copies ran while one was open for 2% of the time, Pallas kernels for 19%

commit v1 on v0

--- a/solution.py
+++ b/solution.py
@@ -16,6 +16,7 @@
 VISCOSITY = 0.25
 VMEM_BYTES = 63 * 1024 * 1024
 NO_COST = pl.CostEstimate(flops=0, bytes_accessed=0, transcendentals=0)
+HIGH_COST = pl.CostEstimate(flops=10**12, bytes_accessed=10**9, transcendentals=0)
 
 
 def params(steps):
@@ -26,6 +27,10 @@
 
 def unit_lanes(width):
     return LANES if width % LANES == 0 else width
+
+
+def even(kept):
+    return kept + kept % 2
 
 
 def step_rows(rows):
@@ -87,7 +92,7 @@
         for start in range(0, ROWS, HALF):
             flat = ref[pl.ds(first + start, HALF)].reshape(HALF * planes, width)
             part = jnp.dot(chosen[...], flat, preferred_element_type=jnp.float32)
-            picked.append(part.reshape(kept, HALF, width))
+            picked.append(part.reshape(-1, HALF, width)[:kept])
         return jnp.concatenate(picked, axis=1).astype(jnp.bfloat16)
 
     def some(index, carry):
@@ -138,7 +143,7 @@
         + [pl.BlockSpec((others, 2, group, lanes), lambda i: (0, 0, i, 0))] * halves,
         scratch_shapes=[
             pltpu.SMEM((planes,), jnp.int32),
-            pltpu.VMEM((kept * HALF, HALF * planes), jnp.bfloat16),
+            pltpu.VMEM((even(kept) * HALF, HALF * planes), jnp.bfloat16),
             pltpu.VMEM((max(others, 1), ROWS, width), jnp.bfloat16),
         ],
         compiler_params=params(1),
@@ -200,7 +205,7 @@
         fields = jnp.concatenate([u, flux], axis=0)
         acc = jnp.dot(bands[0], fields, preferred_element_type=jnp.float32)
         acc = acc + jnp.dot(bands[1], fields, preferred_element_type=jnp.float32)
-        out_ref[:, here] = acc.reshape(kept, HALF, width)
+        out_ref[:, here] = acc.reshape(-1, HALF, width)[:kept]
         return carry
 
     lax.fori_loop(0, rows // HALF, some, 0)
@@ -222,7 +227,7 @@
         out_specs=pl.BlockSpec((kept, group, width), lambda i: (0, i, 0)),
         scratch_shapes=[
             pltpu.SMEM((planes,), jnp.int32),
-            pltpu.VMEM((2, kept * HALF, 2 * HALF * planes), jnp.bfloat16),
+            pltpu.VMEM((2, even(kept) * HALF, 2 * HALF * planes), jnp.bfloat16),
         ],
         compiler_params=params(1),
         cost_estimate=NO_COST,
@@ -318,92 +323,114 @@
     return blocks, jnp.stack(spots).astype(jnp.int32)
 
 
-def wall_kernel(whole_steps, spot_ref, matrix_ref, pair_ref, *refs):
-    *half_refs, out_ref, lines = refs
+def with_flux(pair):
+    u, v = pair
+    return u, (u.astype(jnp.float32) * v.astype(jnp.float32)).astype(jnp.bfloat16)
+
+
+def abreast(group):
+    return 2 if group % 2 == 0 else 1
+
+
+def units_a_step(units):
+    return next(g for g in (4, 6, 10, 2, 1) if units % g == 0)
+
+
+def whole_kernel(matrix_ref, pair_ref, _, out_ref, lines):
     sources, group, _, rows, lanes = pair_ref.shape
     total = sources * rows
-    step = pl.program_id(0)
-    pack_units = 2 if group % 2 == 0 else 1
-
-    def both(u, v):
-        return u, (u.astype(jnp.float32) * v.astype(jnp.float32)).astype(jnp.bfloat16)
-
-    def put(unit, terms):
+    side = abreast(group)
+
+    def some(index, carry):
+        for k in range(side):
+            unit = index * side + k
+            lane = slice(k * lanes, (k + 1) * lanes)
+            u, flux = with_flux((pair_ref[:, unit, 0], pair_ref[:, unit, 1]))
+            lines[:total, lane] = u.reshape(total, lanes)
+            lines[total:, lane] = flux.reshape(total, lanes)
+        terms = jnp.dot(matrix_ref[...], lines[...], preferred_element_type=jnp.float32)
         terms = terms.astype(jnp.bfloat16)
-        for k in range(pack_units):
+        for k in range(side):
             lane = slice(k * lanes, (k + 1) * lanes)
-            out_ref[:, unit + k] = terms[:, lane].reshape(sources, rows, lanes)
-
-    @pl.when(step < whole_steps)
-    def _():
-        def some(index, carry):
-            unit = index * pack_units
-            for k in range(pack_units):
-                u, flux = both(pair_ref[:, unit + k, 0], pair_ref[:, unit + k, 1])
+            out_ref[:, index * side + k] = terms[:, lane].reshape(sources, rows, lanes)
+        return carry
+
+    lax.fori_loop(0, group // side, some, 0)
+
+
+def whole_terms(matrix, pairs, behind):
+    sources, units, _, rows, lanes = pairs.shape
+    group = units_a_step(units)
+    return pl.pallas_call(
+        whole_kernel,
+        grid=(units // group,),
+        out_shape=jax.ShapeDtypeStruct(behind.shape, behind.dtype),
+        in_specs=[
+            pl.BlockSpec(matrix.shape, lambda i: (0, 0)),
+            pl.BlockSpec((sources, group, 2, rows, lanes), lambda i: (0, i, 0, 0, 0)),
+            pl.BlockSpec(memory_space=pl.ANY),
+        ],
+        out_specs=pl.BlockSpec((sources, group, rows, lanes), lambda i: (0, i, 0, 0)),
+        scratch_shapes=[pltpu.VMEM((2 * sources * rows, abreast(group) * lanes), jnp.bfloat16)],
+        input_output_aliases={2: 0},
+        compiler_params=params(1),
+        cost_estimate=NO_COST,
+        name="whole_terms",
+    )(matrix, pairs, behind)
+
+
+def half_kernel(spot_ref, matrix_ref, *refs):
+    *pair_refs, out_ref, lines = refs
+    group, _, rows, lanes = pair_refs[0].shape
+    side = abreast(group)
+    half = len(pair_refs) * rows
+    on_u = pl.ds(pl.multiple_of(spot_ref[1] * half, half), half)
+    on_flux = pl.ds(pl.multiple_of((2 + spot_ref[1]) * half, half), half)
+
+    def some(index, carry):
+        for mask, ref in enumerate(pair_refs):
+            start = pl.multiple_of((spot_ref[0] ^ mask) * rows, rows)
+            for k in range(side):
+                unit = index * side + k
                 lane = slice(k * lanes, (k + 1) * lanes)
-                lines[:total, lane] = u.reshape(total, lanes)
-                lines[total:, lane] = flux.reshape(total, lanes)
-            put(unit, jnp.dot(matrix_ref[...], lines[...], preferred_element_type=jnp.float32))
-            return carry
-
-        lax.fori_loop(0, group // pack_units, some, 0)
-
-    if len(half_refs) == 0:
-        return
-    near = total // 2
-
-    @pl.when(step >= whole_steps)
-    def _():
-        def some(index, carry):
-            unit = index * pack_units
-            for mask, ref in enumerate(half_refs):
-                start = pl.multiple_of((spot_ref[0] ^ mask) * rows, rows)
-                for k in range(pack_units):
-                    u, flux = both(ref[unit + k, 0], ref[unit + k, 1])
-                    lane = slice(k * lanes, (k + 1) * lanes)
-                    lines[pl.ds(start, rows), lane] = u
-                    lines[pl.ds(start + near, rows), lane] = flux
-            on_u = pl.ds(pl.multiple_of(spot_ref[1] * near, near), near)
-            on_flux = pl.ds(pl.multiple_of(total + spot_ref[1] * near, near), near)
-            terms = jnp.dot(
-                matrix_ref[:, on_u], lines[:near], preferred_element_type=jnp.float32
-            ) + jnp.dot(
-                matrix_ref[:, on_flux], lines[near : 2 * near], preferred_element_type=jnp.float32
-            )
-            put(unit, terms)
-            return carry
-
-        lax.fori_loop(0, group // pack_units, some, 0)
-
-
-def wall_terms(spot, matrix, pairs, halves):
-    sources, units, _, rows, lanes = pairs.shape
-    more = halves[0].shape[0] if halves else 0
-    group = next(g for g in (4, 6, 10, 2, 1) if units % g == 0)
-    whole_steps = units // group
-    pack_units = 2 if group % 2 == 0 else 1
-    half_blocks = [
-        pl.BlockSpec((group, 2, rows, lanes), lambda i: (jnp.maximum(i - whole_steps, 0), 0, 0, 0))
-    ] * len(halves)
+                u, flux = with_flux((ref[unit, 0], ref[unit, 1]))
+                lines[pl.ds(start, rows), lane] = u
+                lines[pl.ds(pl.multiple_of(half + start, rows), rows), lane] = flux
+        terms = jnp.dot(matrix_ref[:, on_u], lines[:half], preferred_element_type=jnp.float32)
+        terms = terms + jnp.dot(
+            matrix_ref[:, on_flux], lines[half:], preferred_element_type=jnp.float32
+        )
+        terms = terms.astype(jnp.bfloat16)
+        for k in range(side):
+            lane = slice(k * lanes, (k + 1) * lanes)
+            out_ref[:, index * side + k] = terms[:, lane].reshape(-1, rows, lanes)
+        return carry
+
+    lax.fori_loop(0, group // side, some, 0)
+
+
+def half_terms(spot, matrix, pairs, before):
+    near = len(pairs)
+    units, _, rows, lanes = pairs[0].shape
+    group = units_a_step(before)
+    side = abreast(group)
     return pl.pallas_call(
-        functools.partial(wall_kernel, whole_steps),
-        grid=(whole_steps + pl.cdiv(more, group),),
-        out_shape=jax.ShapeDtypeStruct((sources, units + more, rows, lanes), jnp.bfloat16),
+        half_kernel,
+        grid=(pl.cdiv(units, group),),
+        out_shape=jax.ShapeDtypeStruct((2 * near, before + units, rows, lanes), jnp.bfloat16),
         in_specs=[
             pl.BlockSpec(memory_space=pltpu.SMEM),
             pl.BlockSpec(matrix.shape, lambda i: (0, 0)),
-            pl.BlockSpec(
-                (sources, group, 2, rows, lanes),
-                lambda i: (0, jnp.minimum(i, whole_steps - 1), 0, 0, 0),
-            ),
         ]
-        + half_blocks,
-        out_specs=pl.BlockSpec((sources, group, rows, lanes), lambda i: (0, i, 0, 0)),
-        scratch_shapes=[pltpu.VMEM((2 * sources * rows, pack_units * lanes), jnp.bfloat16)],
+        + [pl.BlockSpec((group, 2, rows, lanes), lambda i: (i, 0, 0, 0))] * near,
+        out_specs=pl.BlockSpec(
+            (2 * near, group, rows, lanes), lambda i: (0, before // group + i, 0, 0)
+        ),
+        scratch_shapes=[pltpu.VMEM((2 * near * rows, side * lanes), jnp.bfloat16)],
         compiler_params=params(1),
-        cost_estimate=NO_COST,
-        name="wall_terms",
-    )(spot, matrix, pairs, *halves)
+        cost_estimate=HIGH_COST,
+        name="half_terms",
+    )(spot, matrix, *pairs)
 
 
 def finish_kernel(apart, counts_ref, base_ref, wall_ref, out_ref, order, chosen, placed):
@@ -432,8 +459,10 @@
                 column = jnp.concatenate([column, low + high], axis=0)
             columns.append(column)
         value = base_ref[:, here] + jnp.concatenate(columns, axis=-1)
+        if kept % 2 == 1:
+            value = jnp.concatenate([value, jnp.zeros((1, ROWS, width), jnp.float32)], axis=0)
         for start in range(0, ROWS, HALF):
-            some_rows = value[:, start : start + HALF].reshape(kept * HALF, width)
+            some_rows = value[:, start : start + HALF].reshape(-1, width)
             out = jnp.dot(
                 placed[...], some_rows.astype(jnp.bfloat16), preferred_element_type=jnp.float32
             )
@@ -461,8 +490,8 @@
         out_specs=pl.BlockSpec((group, planes, width), lambda i: (i, 0, 0)),
         scratch_shapes=[
             pltpu.SMEM((planes,), jnp.int32),
-            pltpu.VMEM((kept * HALF, HALF * planes), jnp.bfloat16),
-            pltpu.VMEM((HALF * planes, kept * HALF), jnp.bfloat16),
+            pltpu.VMEM((even(kept) * HALF, HALF * planes), jnp.bfloat16),
+            pltpu.VMEM((HALF * planes, even(kept) * HALF), jnp.bfloat16),
         ],
         compiler_params=params(1),
         cost_estimate=NO_COST,
@@ -488,17 +517,23 @@
     own, pairs, *halves = pack(counts, spot, u, v, apart, kept, near)
     parts, _, _, _, lanes = pairs.shape
     units = parts * apart // columns
+    halves = [swap(half, mask) for mask, half in enumerate(halves)]
+    if halves:
+        pairs, halves[1] = lax.optimization_barrier((pairs, halves[1]))
     lines = lax.all_to_all(
         pairs.reshape(columns, units, 2, rows, lanes), "col", split_axis=0, concat_axis=0
     )
-    halves = [swap(half, mask) for mask, half in enumerate(halves)]
     one, two = metric1[:, None], metric2[:, None]
     wide_first = wall_first.astype(jnp.float32)
     on_stream = VISCOSITY * (one * one * wall_second.astype(jnp.float32) + two * wide_first)
     matrix = jnp.concatenate([on_stream, -one * wide_first], axis=1).astype(jnp.bfloat16)
     first_block = swap_rows(own, lax.axis_size("row") // 2)
-    lines, halves, first_block = lax.optimization_barrier((lines, halves, first_block))
-    wall = wall_terms(spot, matrix, lines, halves)
+    if halves:
+        wall = half_terms(spot, matrix, halves, units)
+    else:
+        wall = jnp.zeros((columns, units, rows, lanes), jnp.bfloat16)
+    lines, wall, first_block = lax.optimization_barrier((lines, wall, first_block))
+    wall = whole_terms(matrix, lines, wall)
     wall = lax.all_to_all(wall, "col", split_axis=0, concat_axis=0)
     blocks, spots = gather_rows(own, first_block)
     span = span_terms(counts, coef, u, w, kept)
@@ -510,7 +545,7 @@
     if 2 * parts != columns:
         return kept
     options = range(columns // 2, kept + 1, columns // 2)
-    return min(options, key=lambda a: max(2 * a, 1.5 * a + kept - a) + a + 2 * (kept - a))
+    return min(options, key=lambda a: max(12 + 2 * a, 2 + kept + a / 2) - 1.01 * a)
 
 
 def on_device(u, v, w, first, second, wall_first, wall_second, metric1, metric2, coef, counts):
@@ -518,11 +553,11 @@
     planes, width = u.shape[1:]
     columns = lax.axis_size("col")
     parts = width // unit_lanes(width)
-    step = 2 if 2 * parts == columns else columns // math.gcd(columns, parts)
+    step = 1 if 2 * parts == columns else columns // math.gcd(columns, parts)
     blocks = counts.shape[0]
     least, middle = blocks - 1 + ZB, (blocks - 1) * (ZB + 1) / 2 + ZB
     sizes = [size for size in range(step, planes, step) if size >= least]
-    sizes = [size for size in sizes if abs(size - middle) < 3.5 * step] + [planes]
+    sizes = [size for size in sizes if -4 < (size - middle) / step < 6] + [planes]
     branches = [
         functools.partial(with_kept, share_of(size, parts, columns), size) for size in sizes
     ]

time: 128 us -> 123 us (0.961)
  waiting for transfers between devices: 63.5 us -> 51.9 us
  Pallas kernels: 41.9 us -> 44.5 us
  starting transfers between devices: 17.6 us -> 20.1 us
    ppermute x3, waiting for transfers between devices: 39.5 us -> 14.5 us  [swap(): lax.ppermute(array, 'col', [(column, column ^ mask) for column in range(c...]
    all_to_all x1, waiting for transfers between devices: 21.8 us -> 28.8 us  [with_kept(): wall = lax.all_to_all(wall, 'col', split_axis=0, concat_axis=0)]
    ppermute x3, waiting for transfers between devices: 0.01 us -> 3.46 us  [swap_rows(): lax.ppermute(array, 'row', [(row, row ^ mask) for row in range(count)])]
    all_to_all x1, waiting for transfers between devices: 2.15 us -> 5.15 us  [with_kept(): lax.all_to_all(pairs.reshape(columns, units, 2, rows, lanes), 'col', spli...]
    pallas_call x1 -> x2, Pallas kernels: 6.56 us -> 9.06 us  [the longest x1 5.73 us: half_terms(): pl.pallas_call(half_kernel, grid=(pl.cdiv(units, group),), out_shape=jax....]
    all_to_all x1, starting transfers between devices: 4.51 us -> 6.72 us  [with_kept(): wall = lax.all_to_all(wall, 'col', split_axis=0, concat_axis=0)]
  transfers between devices with their start and end apart: 8 -> 8, of which waited for: 5 -> 5; matrix products, arithmetic and copies ran while one was open for 2% -> 3% of each run, Pallas kernels for 19% -> 25%
where the time goes in v1:
time: 123 us; the launch traced here: 122 us
  waiting for transfers between devices  51.9 us (42%)
  Pallas kernels  44.5 us (36%)
  starting transfers between devices  20.1 us (16%)
  other arithmetic  5.06 us (4%)
    all_to_all x1, waiting for transfers between devices, with_kept(): wall = lax.all_to_all(wall, 'col', split_axis=0, concat_axis=0)  28.8 us
    pallas_call x1, Pallas kernels, stream_terms(): pl.pallas_call(stream_kernel, grid=(pl.cdiv(kept, group),), out_shape=jax...  17.6 us
    ppermute x3, waiting for transfers between devices, swap(): lax.ppermute(array, 'col', [(column, column ^ mask) for column in range(c...  14.5 us
    pallas_call x1, Pallas kernels, span_terms(): pl.pallas_call(span_kernel, grid=(rows // group,), out_shape=jax.ShapeDty...  7.12 us
    all_to_all x1, starting transfers between devices, with_kept(): wall = lax.all_to_all(wall, 'col', split_axis=0, concat_axis=0)  6.72 us
    all_to_all x1, starting transfers between devices, with_kept(): lax.all_to_all(pairs.reshape(columns, units, 2, rows, lanes), 'col', spli...  6.34 us
    pallas_call x1, Pallas kernels, half_terms(): pl.pallas_call(half_kernel, grid=(pl.cdiv(units, group),), out_shape=jax....  5.73 us
    pallas_call x1, Pallas kernels, pack(): pl.pallas_call(pack_kernel, grid=(rows // group,), out_shape=[jax.ShapeDt...  5.62 us
  transfers between devices with their start and end apart: 8, of which 5 were waited for; matrix products, arithmetic and copies ran while one was open for 3% of the time, Pallas kernels for 25%

profile of v1, /device:TPU:0, one launch (start us, length us, event | category | flops | bytes accessed | tf_op | source)
XLA Modules:
  0.0 122.5 jit_solution(7982533662655714358)
XLA Ops:
  0.0 1.3 %reduce_sum.9 = s32[]{:T(128)} reduce(s32[8]{0:T(128)} %param.32, s32[]{:T(128)} %constant.391.clone.1), dimensions={0}, to_apply=%region_0.0 | reduce | flops 7 | bytes 40 | tf_op jit(solution)/shard_map/reduce_sum | solution.py:564
  1.9 120.5 %conditional.1 = (bf16[64,32,512]{2,1,0:T(8,128)(2,1)}) conditional(s32[]{:T(128)} %clamp.3, (s32[8]{0:T(128)}, bf16[64,32,512]{2,1,0:T(8,128)(2,1)}, bf16[64,32,512]{2,1,0:T(8,128)(2,1)}, f32[512]{0:T(512)}, bf16[512,512]{1,0:T(8,128)(2,1)}, /*index=5*/f32[512]{0:T(512)}, bf16[512,512]{1,0:T(8,128)(2,1)}, ...), branch_computations={%region_1.2_spmd, %region_2.3_spmd, %region_3.4_spmd, %region_4.5_... | conditional | flops 1000004452352 | bytes 1053507200 | solution.py:567
  2.2 0.6 pad_add_fusion.11.spot_ref
  2.8 5.6 %pack.16 = (bf16[23,64,512]{2,1,0:T(8,128)(2,1)}, bf16[4,8,2,64,128]{4,3,2,1,0:T(8,128)(2,1)}, bf16[15,2,64,128]{3,2,1,0:T(8,128)(2,1)}, bf16[15,2,64,128]{3,2,1...) custom-call(s32[8]{0:T(128)} %get-tuple-element.369.counts_ref, ...), custom_call_target="tpu_custom_call" | custom-call | tf_op jit(solution)/shard_map/cond/branch_5_fun/pack/pallas_call | solution.py:125
  8.4 3.0 %collective-permute-start.30 = (bf16[15,2,64,128]{3,2,1,0:T(8,128)(2,1)}, bf16[15,2,64,128]{3,2,1,0:T(8,128)(2,1)}, u32[]{:S(2)}, u32[]{:S(2)}) collective-permute-start(bf16[15,2,64,128]{3,2,1,0:T(8,128)(2,1)} %get-tuple-element.374), channel_id=1, source_target_pairs={{0,1},{1,0},{2,3},{3,2},{4,5},{5,4},{6,7},{7,6},{8,9},{9,8},{10,11... | collective-permute-start | bytes 1474568 | tf_op jit(solution)/shard_map/cond/branch_5_fun/ppermute | solution.py:506
  11.4 1.6 %collective-permute-start.31 = (bf16[15,2,64,128]{3,2,1,0:T(8,128)(2,1)}, bf16[15,2,64,128]{3,2,1,0:T(8,128)(2,1)}, u32[]{:S(2)}, u32[]{:S(2)}) collective-permute-start(bf16[15,2,64,128]{3,2,1,0:T(8,128)(2,1)} %get-tuple-element.382), channel_id=1, source_target_pairs={{0,2},{1,3},{2,0},{3,1},{4,6},{5,7},{6,4},{7,5},{8,10},{9,11},{10,... | collective-permute-start | bytes 1474568 | tf_op jit(solution)/shard_map/cond/branch_5_fun/ppermute | solution.py:506
  13.0 0.0 collective-permute-start.32
  13.0 1.9 %collective-permute-start.33 = (bf16[23,64,512]{2,1,0:T(8,128)(2,1)}, bf16[23,64,512]{2,1,0:T(8,128)(2,1)}, u32[]{:S(2)}, u32[]{:S(2)}) collective-permute-start(bf16[23,64,512]{2,1,0:T(8,128)(2,1)} %get-tuple-element.372.refs_0_), channel_id=1, source_target_pairs={{0,16},{8,24},{16,0},{24,8},{1,17},{9,25},{17,1},{25,9},{2,18},{10... | collective-permute-start | bytes 4521992 | tf_op jit(solution)/shard_map/cond/branch_5_fun/ppermute | solution.py:312
  14.9 0.0 copy-done.38
  14.9 0.0 copy-done.5
  14.9 0.0 copy-done.27
  14.9 1.4 %fusion.22 = (bf16[512,512]{1,0:T(8,128)(2,1)S(1)}, bf16[512,512]{1,0:T(8,128)(2,1)S(1)}) fusion(bf16[512,512]{1,0:T(8,128)(2,1)} %get-tuple-element.379, bf16[512,512]{1,0:T(8,128)(2,1)S(1)} %copy-done.5, f32[512]{0:T(512)S(1)} %copy-done.27, f32[512]{0:T(512)S(1)} %get-tuple-element.524, f32[512]{0:T(512)S(1)} %get-tuple-element.523), kind=kLoop, calls=%fused_computation.49 | loop fusion | flops 2359296 | bytes 2103296 | tf_op jit(solution)/shard_map/convert.10
  16.3 1.1 pad_maximum_fusion.5.matrix_ref
  17.5 5.5 %collective-permute-done.30.refs_1_ = bf16[15,2,64,128]{3,2,1,0:T(8,128)(2,1)} collective-permute-done((bf16[15,2,64,128]{3,2,1,0:T(8,128)(2,1)}, bf16[15,2,64,128]{3,2,1,0:T(8,128)(2,1)}, u32[]{:S(2)}, u32[]{:S(2)}) %collective-permute-start.30) | collective-permute-done | bytes 491552 | tf_op jit(solution)/shard_map/cond/branch_5_fun/ppermute | solution.py:506
  22.9 6.3 %all-to-all-start.10 = ((bf16[8,4,2,64,128]{4,3,2,1,0:T(8,128)(2,1)}), bf16[8,4,2,64,128]{4,3,2,1,0:T(8,128)(2,1)}, u32[]{:S(2)}, u32[]{:S(2)}) async-start(bf16[8,4,2,64,128]{4,3,2,1,0:T(8,128)(2,1)} %bitcast.41), calls=%async_computation.10 | async-start | bytes 2097152 | tf_op jit(solution)/shard_map/cond/branch_5_fun/all_to_all | solution.py:523
  29.3 0.0 collective-permute-done.31.refs_2_
  29.3 9.0 %collective-permute-done.32.refs_3_ = bf16[15,2,64,128]{3,2,1,0:T(8,128)(2,1)} collective-permute-done((bf16[15,2,64,128]{3,2,1,0:T(8,128)(2,1)}, bf16[15,2,64,128]{3,2,1,0:T(8,128)(2,1)}, u32[]{:S(2)}, u32[]{:S(2)}) %collective-permute-start.32) | collective-permute-done | bytes 491552 | tf_op jit(solution)/shard_map/cond/branch_5_fun/ppermute | solution.py:506
  38.3 5.7 %half_terms.16._ = bf16[8,19,64,128]{3,2,1,0:T(8,128)(2,1)} custom-call(s32[2]{0:T(128)} %pad_add_fusion.11.spot_ref, bf16[512,1024]{1,0:T(8,128)(2,1)} %pad_maximum_fusion.5.matrix_ref, bf16[15,2,64,128]{3,2,1,0:T(8,128)(2,1)} %get-tuple-element.380.refs_0_, bf16[15,2,64,128]{3,2,1,0:T(8,128)(2,1)} %collective-permute-done.30.refs_1_, ...), custom_call_target="tpu_custom_call" | custom-call | flops 999999995904 | bytes 1000000000 | tf_op jit(solution)/shard_map/cond/branch_5_fun/half_terms/pallas_call | solution.py:417
  44.0 3.5 %collective-permute-done.33.refs_1_ = bf16[23,64,512]{2,1,0:T(8,128)(2,1)} collective-permute-done((bf16[23,64,512]{2,1,0:T(8,128)(2,1)}, bf16[23,64,512]{2,1,0:T(8,128)(2,1)}, u32[]{:S(2)}, u32[]{:S(2)}) %collective-permute-start.33) | collective-permute-done | bytes 1507360 | tf_op jit(solution)/shard_map/cond/branch_5_fun/ppermute | solution.py:312
  47.5 5.1 %all-to-all-done.10.pair_ref = bf16[8,4,2,64,128]{4,3,2,1,0:T(8,128)(2,1)} async-done(((bf16[8,4,2,64,128]{4,3,2,1,0:T(8,128)(2,1)}), bf16[8,4,2,64,128]{4,3,2,1,0:T(8,128)(2,1)}, u32[]{:S(2)}, u32[]{:S(2)}) %all-to-all-start.10) | async-done | bytes 1048608 | tf_op jit(solution)/shard_map/cond/branch_5_fun/all_to_all | solution.py:523
  52.6 3.3 %whole_terms.16 = bf16[8,19,64,128]{3,2,1,0:T(8,128)(2,1)} custom-call(bf16[512,1024]{1,0:T(8,128)(2,1)} %pad_maximum_fusion.5.matrix_ref, bf16[8,4,2,64,128]{4,3,2,1,0:T(8,128)(2,1)} %all-to-all-done.10.pair_ref, bf16[8,19,64,128]{3,2,1,0:T(8,128)(2,1)} %half_terms.16._), custom_call_target="tpu_custom_call", output_to_operand_aliasing={{}: (2, {})} | custom-call | tf_op jit(solution)/shard_map/cond/branch_5_fun/whole_terms/pallas_call | solution.py:364
  56.0 6.7 %all-to-all-start.11 = ((bf16[8,19,64,128]{3,2,1,0:T(8,128)(2,1)}), bf16[8,19,64,128]{3,2,1,0:T(8,128)(2,1)}, u32[]{:S(2)}, u32[]{:S(2)}) async-start(bf16[8,19,64,128]{3,2,1,0:T(8,128)(2,1)} %whole_terms.16), calls=%async_computation.11 | async-start | bytes 4980736 | tf_op jit(solution)/shard_map/cond/branch_5_fun/all_to_all | solution.py:537
  62.7 0.0 collective-permute-start.34
  62.7 0.5 collective-permute-start.35
  63.2 0.0 copy-done.16
  63.2 7.1 %span_terms.16.refs_6_ = f32[23,64,512]{2,1,0:T(8,128)} custom-call(s32[8]{0:T(128)S(1)} %copy-done.16, f32[2,9]{1,0:T(2,128)S(1)} %copy-done.49, bf16[64,32,512]{2,1,0:T(8,128)(2,1)} %get-tuple-element.370.u_ref, bf16[64,32,512]{2,1,0:T(8,128)(2,1)} %get-tuple-element.388.w_ref), custom_call_target="tpu_custom_call" | custom-call | tf_op jit(solution)/shard_map/cond/branch_5_fun/span_terms/pallas_call | solution.py:217
  70.3 0.7 pad_add_fusion.10.spots_ref
  71.0 0.0 collective-permute-done.34.refs_2_
  71.0 0.0 collective-permute-done.35.refs_3_
  71.0 17.6 %stream_terms.16.base_ref = f32[23,64,512]{2,1,0:T(8,128)} custom-call(s32[4]{0:T(128)} %pad_add_fusion.10.spots_ref, bf16[23,64,512]{2,1,0:T(8,128)(2,1)} %get-tuple-element.372.refs_0_, bf16[23,64,512]{2,1,0:T(8,128)(2,1)} %collective-permute-done.33.refs_1_, bf16[23,64,512]{2,1,0:T(8,128)(2,1)} %collective-permute-done.34.refs_2_, ...), custom_call_target="tpu_custom_call" | custom-call | tf_op jit(solution)/shard_map/cond/branch_5_fun/stream_terms/pallas_call | solution.py:292
  88.6 28.8 %all-to-all-done.11.wall_ref = bf16[8,19,64,128]{3,2,1,0:T(8,128)(2,1)} async-done(((bf16[8,19,64,128]{3,2,1,0:T(8,128)(2,1)}), bf16[8,19,64,128]{3,2,1,0:T(8,128)(2,1)}, u32[]{:S(2)}, u32[]{:S(2)}) %all-to-all-start.11) | async-done | bytes 2490400 | tf_op jit(solution)/shard_map/cond/branch_5_fun/all_to_all | solution.py:537
  117.4 5.1 %finish.16 = bf16[64,32,512]{2,1,0:T(8,128)(2,1)} custom-call(s32[8]{0:T(128)S(1)} %copy-done.16, f32[23,64,512]{2,1,0:T(8,128)} %stream_terms.16.base_ref, bf16[8,19,64,128]{3,2,1,0:T(8,128)(2,1)} %all-to-all-done.11.wall_ref), custom_call_target="tpu_custom_call" | custom-call | tf_op jit(solution)/shard_map/cond/branch_5_fun/finish/pallas_call | solution.py:481
  (7 shorter events, 0.0 us)
Async XLA Ops:
  2.8 12.1 %copy-start.38 = (f32[512]{0:T(512)S(1)}, f32[512]{0:T(512)}, u32[]{:S(2)}) copy-start(f32[512]{0:T(512)} %get-tuple-element.376) | copy-start | bytes 6148 | tf_op jit(solution)/shard_map/cond
  2.8 12.1 %copy-start.5 = (bf16[512,512]{1,0:T(8,128)(2,1)S(1)}, bf16[512,512]{1,0:T(8,128)(2,1)}, u32[]{:S(2)}) copy-start(bf16[512,512]{1,0:T(8,128)(2,1)} %get-tuple-element.377) | copy-start | bytes 1572868 | tf_op jit(solution)/shard_map/cond
  2.8 12.1 %copy-start.27 = (f32[512]{0:T(512)S(1)}, f32[512]{0:T(512)}, u32[]{:S(2)}) copy-start(f32[512]{0:T(512)} %get-tuple-element.378) | copy-start | bytes 6148 | tf_op jit(solution)/shard_map/cond
  8.4 14.5 %collective-permute-start.30 = (bf16[15,2,64,128]{3,2,1,0:T(8,128)(2,1)}, bf16[15,2,64,128]{3,2,1,0:T(8,128)(2,1)}, u32[]{:S(2)}, u32[]{:S(2)}) collective-permute-start(bf16[15,2,64,128]{3,2,1,0:T(8,128)(2,1)} %get-tuple-element.374), channel_id=1, source_target_pairs={{0,1},{1,0},{2,3},{3,2},{4,5},{5,4},{6,7},{7,6},{8,9},{9,8},{10,11... | collective-permute-start | bytes 1474568 | tf_op jit(solution)/shard_map/cond/branch_5_fun/ppermute | solution.py:506
  11.4 17.9 %collective-permute-start.31 = (bf16[15,2,64,128]{3,2,1,0:T(8,128)(2,1)}, bf16[15,2,64,128]{3,2,1,0:T(8,128)(2,1)}, u32[]{:S(2)}, u32[]{:S(2)}) collective-permute-start(bf16[15,2,64,128]{3,2,1,0:T(8,128)(2,1)} %get-tuple-element.382), channel_id=1, source_target_pairs={{0,2},{1,3},{2,0},{3,1},{4,6},{5,7},{6,4},{7,5},{8,10},{9,11},{10,... | collective-permute-start | bytes 1474568 | tf_op jit(solution)/shard_map/cond/branch_5_fun/ppermute | solution.py:506
  13.0 25.3 %collective-permute-start.32 = (bf16[15,2,64,128]{3,2,1,0:T(8,128)(2,1)}, bf16[15,2,64,128]{3,2,1,0:T(8,128)(2,1)}, u32[]{:S(2)}, u32[]{:S(2)}) collective-permute-start(bf16[15,2,64,128]{3,2,1,0:T(8,128)(2,1)} %get-tuple-element.383), channel_id=1, source_target_pairs={{0,3},{1,2},{2,1},{3,0},{4,7},{5,6},{6,5},{7,4},{8,11},{9,10},{10,... | collective-permute-start | bytes 1474568 | tf_op jit(solution)/shard_map/cond/branch_5_fun/ppermute | solution.py:506
  13.0 34.5 %collective-permute-start.33 = (bf16[23,64,512]{2,1,0:T(8,128)(2,1)}, bf16[23,64,512]{2,1,0:T(8,128)(2,1)}, u32[]{:S(2)}, u32[]{:S(2)}) collective-permute-start(bf16[23,64,512]{2,1,0:T(8,128)(2,1)} %get-tuple-element.372.refs_0_), channel_id=1, source_target_pairs={{0,16},{8,24},{16,0},{24,8},{1,17},{9,25},{17,1},{25,9},{2,18},{10... | collective-permute-start | bytes 4521992 | tf_op jit(solution)/shard_map/cond/branch_5_fun/ppermute | solution.py:312
  22.9 29.7 %all-to-all-start.10 = ((bf16[8,4,2,64,128]{4,3,2,1,0:T(8,128)(2,1)}), bf16[8,4,2,64,128]{4,3,2,1,0:T(8,128)(2,1)}, u32[]{:S(2)}, u32[]{:S(2)}) async-start(bf16[8,4,2,64,128]{4,3,2,1,0:T(8,128)(2,1)} %bitcast.41), calls=%async_computation.10 | async-start | bytes 2097152 | tf_op jit(solution)/shard_map/cond/branch_5_fun/all_to_all | solution.py:523
  56.0 7.2 %copy-start.16 = (s32[8]{0:T(128)S(1)}, s32[8]{0:T(128)}, u32[]{:S(2)}) copy-start(s32[8]{0:T(128)} %get-tuple-element.369.counts_ref) | copy-start | bytes 100 | tf_op jit(solution)/shard_map/cond
  56.0 7.2 %copy-start.49 = (f32[2,9]{1,0:T(2,128)S(1)}, f32[2,9]{1,0:T(2,128)}, u32[]{:S(2)}) copy-start(f32[2,9]{1,0:T(2,128)} %get-tuple-element.387.coef_ref) | copy-start | bytes 220 | tf_op jit(solution)/shard_map/cond
  56.0 61.4 %all-to-all-start.11 = ((bf16[8,19,64,128]{3,2,1,0:T(8,128)(2,1)}), bf16[8,19,64,128]{3,2,1,0:T(8,128)(2,1)}, u32[]{:S(2)}, u32[]{:S(2)}) async-start(bf16[8,19,64,128]{3,2,1,0:T(8,128)(2,1)} %whole_terms.16), calls=%async_computation.11 | async-start | bytes 4980736 | tf_op jit(solution)/shard_map/cond/branch_5_fun/all_to_all | solution.py:537
  62.7 8.3 %collective-permute-start.34 = (bf16[23,64,512]{2,1,0:T(8,128)(2,1)}, bf16[23,64,512]{2,1,0:T(8,128)(2,1)}, u32[]{:S(2)}, u32[]{:S(2)}) collective-permute-start(bf16[23,64,512]{2,1,0:T(8,128)(2,1)} %get-tuple-element.372.refs_0_), channel_id=1, source_target_pairs={{0,8},{8,0},{16,24},{24,16},{1,9},{9,1},{17,25},{25,17},{2,10},{10... | collective-permute-start | bytes 4521992 | tf_op jit(solution)/shard_map/cond/branch_5_fun/ppermute | solution.py:312
  62.7 8.3 %collective-permute-start.35 = (bf16[23,64,512]{2,1,0:T(8,128)(2,1)}, bf16[23,64,512]{2,1,0:T(8,128)(2,1)}, u32[]{:S(2)}, u32[]{:S(2)}) collective-permute-start(bf16[23,64,512]{2,1,0:T(8,128)(2,1)} %collective-permute-done.33.refs_1_), channel_id=1, source_target_pairs={{0,8},{8,0},{16,24},{24,16},{1,9},{9,1},{17,25},{25,17},{2,10},{10... | collective-permute-start | bytes 4521992 | tf_op jit(solution)/shard_map/cond/branch_5_fun/ppermute | solution.py:312

commit v2 on v1

--- a/solution.py
+++ b/solution.py
@@ -507,13 +507,11 @@
 
 
 def with_kept(
-    apart, kept, u, v, w, first, second, wall_first, wall_second, metric1, metric2, coef, counts
+    apart, kept, spot, u, v, w, first, second, wall_first, wall_second, metric1, metric2, coef, counts
 ):
     rows, planes, width = u.shape
     columns = lax.axis_size("col")
-    column = lax.axis_index("col")
     near = columns // 2
-    spot = jnp.stack([column % near, column // near]).astype(jnp.int32)
     own, pairs, *halves = pack(counts, spot, u, v, apart, kept, near)
     parts, _, _, _, lanes = pairs.shape
     units = parts * apart // columns
@@ -557,13 +555,15 @@
     blocks = counts.shape[0]
     least, middle = blocks - 1 + ZB, (blocks - 1) * (ZB + 1) / 2 + ZB
     sizes = [size for size in range(step, planes, step) if size >= least]
-    sizes = [size for size in sizes if -4 < (size - middle) / step < 6] + [planes]
+    sizes = [size for size in sizes if -4 < (size - middle) / step < 5] + [planes]
     branches = [
         functools.partial(with_kept, share_of(size, parts, columns), size) for size in sizes
     ]
     fluid = jnp.sum(counts)
     index = (fluid - sizes[0] + (step - 1)) // step
-    operands = (u, v, w, first, second, wall_first, wall_second, metric1, metric2, coef, counts)
+    column, near = lax.axis_index("col"), columns // 2
+    spot = jnp.stack([column % near, column // near]).astype(jnp.int32)
+    operands = (spot, u, v, w, first, second, wall_first, wall_second, metric1, metric2, coef, counts)
     out = lax.switch(index, branches, *operands)
     return jnp.swapaxes(out, 1, 2)
 

time: 123 us -> 110 us (0.89)
  waiting for transfers between devices: 51.9 us -> 39.4 us
  starting transfers between devices: 20.1 us -> 23 us
  Pallas kernels: 44.5 us -> 42 us
    all_to_all x1, waiting for transfers between devices: 5.15 us -> 0.19 us  [with_kept(): lax.all_to_all(pairs.reshape(columns, units, 2, rows, lanes), 'col', spli...]
    all_to_all x1, waiting for transfers between devices: 28.8 us -> 25 us  [with_kept(): wall = lax.all_to_all(wall, 'col', split_axis=0, concat_axis=0)]
    ppermute x3, waiting for transfers between devices: 3.46 us -> 0.01 us  [swap_rows(): lax.ppermute(array, 'row', [(row, row ^ mask) for row in range(count)])]
    all_to_all x1, starting transfers between devices: 6.72 us -> 9.73 us  [with_kept(): wall = lax.all_to_all(wall, 'col', split_axis=0, concat_axis=0)]
    pallas_call x1, Pallas kernels: 17.6 us -> 15.3 us  [stream_terms(): pl.pallas_call(stream_kernel, grid=(pl.cdiv(kept, group),), out_shape=jax...]
    pallas_call x1, Pallas kernels: 5.73 us -> 7.19 us  [half_terms(): pl.pallas_call(half_kernel, grid=(pl.cdiv(units, group),), out_shape=jax....]
  transfers between devices with their start and end apart: 8 -> 8, of which waited for: 5 -> 4; matrix products, arithmetic and copies ran while one was open for 3% -> 3% of each run, Pallas kernels for 25% -> 27%
where the time goes in v2:
time: 110 us
  Pallas kernels  42 us (38%)
  waiting for transfers between devices  39.4 us (36%)
  starting transfers between devices  23 us (21%)
  other arithmetic  4.43 us (4%)
    all_to_all x1, waiting for transfers between devices, with_kept(): wall = lax.all_to_all(wall, 'col', split_axis=0, concat_axis=0)  25 us
    pallas_call x1, Pallas kernels, stream_terms(): pl.pallas_call(stream_kernel, grid=(pl.cdiv(kept, group),), out_shape=jax...  15.3 us
    ppermute x3, waiting for transfers between devices, swap(): lax.ppermute(array, 'col', [(column, column ^ mask) for column in range(c...  14.3 us
    all_to_all x1, starting transfers between devices, with_kept(): wall = lax.all_to_all(wall, 'col', split_axis=0, concat_axis=0)  9.73 us
    pallas_call x1, Pallas kernels, half_terms(): pl.pallas_call(half_kernel, grid=(pl.cdiv(units, group),), out_shape=jax....  7.19 us
    pallas_call x1, Pallas kernels, span_terms(): pl.pallas_call(span_kernel, grid=(rows // group,), out_shape=jax.ShapeDty...  6.69 us
    all_to_all x1, starting transfers between devices, with_kept(): lax.all_to_all(pairs.reshape(columns, units, 2, rows, lanes), 'col', spli...  6.34 us
    pallas_call x1, Pallas kernels, pack(): pl.pallas_call(pack_kernel, grid=(rows // group,), out_shape=[jax.ShapeDt...  5.32 us
  transfers between devices with their start and end apart: 8, of which 4 were waited for; matrix products, arithmetic and copies ran while one was open for 3% of the time, Pallas kernels for 27%

profile of v2, /device:TPU:0, one launch (start us, length us, event | category | flops | bytes accessed | tf_op | source)
XLA Modules:
  0.0 109.7 jit_solution(17637759083017428704)
XLA Ops:
  0.0 0.1 pad_add_fusion.10
  0.1 1.3 %reduce_sum.9 = s32[]{:T(128)} reduce(s32[8]{0:T(128)} %param.31, s32[]{:T(128)} %constant.146.clone.1), dimensions={0}, to_apply=%region_0.0 | reduce | flops 7 | bytes 40 | tf_op jit(solution)/shard_map/reduce_sum | solution.py:562
  2.0 107.7 %conditional.1 = (bf16[64,32,512]{2,1,0:T(8,128)(2,1)}) conditional(s32[]{:T(128)} %clamp.3, (s32[8]{0:T(128)}, s32[2]{0:T(128)S(1)}, bf16[64,32,512]{2,1,0:T(8,128)(2,1)}, bf16[64,32,512]{2,1,0:T(8,128)(2,1)}, f32[512]{0:T(512)}, /*index=5*/bf16[512,512]{1,0:T(8,128)(2,1)}, f32[512]{0:T(512)}, ...), branch_computations={%region_1.2_spmd, %region_2.3_spmd, %region_3.4_spmd, %region_4.5_... | conditional | flops 1000004452352 | bytes 1053506944 | solution.py:567
  2.0 0.0 copy-start.31
  2.1 0.0 copy-start.1
  2.1 0.0 copy-start.21
  2.1 5.3 %pack.11 = (bf16[19,64,512]{2,1,0:T(8,128)(2,1)}, bf16[4,4,2,64,128]{4,3,2,1,0:T(8,128)(2,1)}, bf16[15,2,64,128]{3,2,1,0:T(8,128)(2,1)}, bf16[15,2,64,128]{3,2,1...) custom-call(s32[8]{0:T(128)} %get-tuple-element.279.counts_ref, ...), custom_call_target="tpu_custom_call" | custom-call | tf_op jit(solution)/shard_map/cond/branch_1_fun/pack/pallas_call | solution.py:125
  7.4 3.0 %collective-permute-start.6 = (bf16[15,2,64,128]{3,2,1,0:T(8,128)(2,1)}, bf16[15,2,64,128]{3,2,1,0:T(8,128)(2,1)}, u32[]{:S(2)}, u32[]{:S(2)}) collective-permute-start(bf16[15,2,64,128]{3,2,1,0:T(8,128)(2,1)} %get-tuple-element.285), channel_id=1, source_target_pairs={{0,1},{1,0},{2,3},{3,2},{4,5},{5,4},{6,7},{7,6},{8,9},{9,8},{10,11... | collective-permute-start | bytes 1474568 | tf_op jit(solution)/shard_map/cond/branch_1_fun/ppermute | solution.py:506
  10.4 1.6 %collective-permute-start.7 = (bf16[15,2,64,128]{3,2,1,0:T(8,128)(2,1)}, bf16[15,2,64,128]{3,2,1,0:T(8,128)(2,1)}, u32[]{:S(2)}, u32[]{:S(2)}) collective-permute-start(bf16[15,2,64,128]{3,2,1,0:T(8,128)(2,1)} %get-tuple-element.293), channel_id=1, source_target_pairs={{0,2},{1,3},{2,0},{3,1},{4,6},{5,7},{6,4},{7,5},{8,10},{9,11},{10,... | collective-permute-start | bytes 1474568 | tf_op jit(solution)/shard_map/cond/branch_1_fun/ppermute | solution.py:506
  11.9 0.0 collective-permute-start.8
  11.9 1.9 %collective-permute-start.9 = (bf16[19,64,512]{2,1,0:T(8,128)(2,1)}, bf16[19,64,512]{2,1,0:T(8,128)(2,1)}, u32[]{:S(2)}, u32[]{:S(2)}) collective-permute-start(bf16[19,64,512]{2,1,0:T(8,128)(2,1)} %get-tuple-element.283.refs_0_), channel_id=1, source_target_pairs={{0,16},{8,24},{16,0},{24,8},{1,17},{9,25},{17,1},{25,9},{2,18},{10... | collective-permute-start | bytes 3735560 | tf_op jit(solution)/shard_map/cond/branch_1_fun/ppermute | solution.py:312
  13.9 0.0 copy-done.1
  13.9 1.4 %fusion.6 = (bf16[512,512]{1,0:T(8,128)(2,1)S(1)}, bf16[512,512]{1,0:T(8,128)(2,1)S(1)}) fusion(bf16[512,512]{1,0:T(8,128)(2,1)} %get-tuple-element.290, bf16[512,512]{1,0:T(8,128)(2,1)S(1)} %copy-done.1, f32[512]{0:T(512)S(1)} %copy-done.21, f32[512]{0:T(512)S(1)} %get-tuple-element.493, f32[512]{0:T(512)S(1)} %get-tuple-element.492), kind=kLoop, calls=%fused_computation.12 | loop fusion | flops 2359296 | bytes 2103296 | tf_op jit(solution)/shard_map/convert.2
  15.3 1.1 %pad_maximum_fusion.1.matrix_ref = bf16[512,1024]{1,0:T(8,128)(2,1)} fusion(bf16[512,512]{1,0:T(8,128)(2,1)S(1)} %get-tuple-element.491, bf16[512,512]{1,0:T(8,128)(2,1)S(1)} %get-tuple-element.490), kind=kLoop, calls=%fused_computation.14 | loop fusion | flops 2097152 | bytes 2097152 | tf_op jit(solution)/shard_map/cond/branch_1_fun/concatenate | solution.py:527
  16.4 5.5 %collective-permute-done.6.refs_1_ = bf16[15,2,64,128]{3,2,1,0:T(8,128)(2,1)} collective-permute-done((bf16[15,2,64,128]{3,2,1,0:T(8,128)(2,1)}, bf16[15,2,64,128]{3,2,1,0:T(8,128)(2,1)}, u32[]{:S(2)}, u32[]{:S(2)}) %collective-permute-start.6) | collective-permute-done | bytes 491552 | tf_op jit(solution)/shard_map/cond/branch_1_fun/ppermute | solution.py:506
  21.9 6.3 %all-to-all-start.2 = ((bf16[8,2,2,64,128]{4,3,2,1,0:T(8,128)(2,1)}), bf16[8,2,2,64,128]{4,3,2,1,0:T(8,128)(2,1)}, u32[]{:S(2)}, u32[]{:S(2)}) async-start(bf16[8,2,2,64,128]{4,3,2,1,0:T(8,128)(2,1)} %bitcast.9), calls=%async_computation.2 | async-start | bytes 1048576 | tf_op jit(solution)/shard_map/cond/branch_1_fun/all_to_all | solution.py:521
  28.2 0.0 collective-permute-done.7.refs_2_
  28.2 8.8 %collective-permute-done.8.refs_3_ = bf16[15,2,64,128]{3,2,1,0:T(8,128)(2,1)} collective-permute-done((bf16[15,2,64,128]{3,2,1,0:T(8,128)(2,1)}, bf16[15,2,64,128]{3,2,1,0:T(8,128)(2,1)}, u32[]{:S(2)}, u32[]{:S(2)}) %collective-permute-start.8) | collective-permute-done | bytes 491552 | tf_op jit(solution)/shard_map/cond/branch_1_fun/ppermute | solution.py:506
  37.0 7.2 %half_terms.11._ = bf16[8,17,64,128]{3,2,1,0:T(8,128)(2,1)} custom-call(s32[2]{0:T(128)S(1)} %get-tuple-element.280.spot_ref, bf16[512,1024]{1,0:T(8,128)(2,1)} %pad_maximum_fusion.1.matrix_ref, bf16[15,2,64,128]{3,2,1,0:T(8,128)(2,1)} %get-tuple-element.291.refs_0_, bf16[15,2,64,128]{3,2,1,0:T(8,128)(2,1)} %collective-permute-done.6.refs_1_, ...), custom_call_target="tpu_custom_call" | custom-call | flops 999999995904 | bytes 1000000000 | tf_op jit(solution)/shard_map/cond/branch_1_fun/half_terms/pallas_call | solution.py:417
  44.2 0.0 collective-permute-done.9.refs_1_
  44.2 0.2 all-to-all-done.2.pair_ref
  44.4 2.5 %whole_terms.11 = bf16[8,17,64,128]{3,2,1,0:T(8,128)(2,1)} custom-call(bf16[512,1024]{1,0:T(8,128)(2,1)} %pad_maximum_fusion.1.matrix_ref, bf16[8,2,2,64,128]{4,3,2,1,0:T(8,128)(2,1)} %all-to-all-done.2.pair_ref, bf16[8,17,64,128]{3,2,1,0:T(8,128)(2,1)} %half_terms.11._), custom_call_target="tpu_custom_call", output_to_operand_aliasing={{}: (2, {})} | custom-call | tf_op jit(solution)/shard_map/cond/branch_1_fun/whole_terms/pallas_call | solution.py:364
  46.9 9.7 %all-to-all-start.3 = ((bf16[8,17,64,128]{3,2,1,0:T(8,128)(2,1)}), bf16[8,17,64,128]{3,2,1,0:T(8,128)(2,1)}, u32[]{:S(2)}, u32[]{:S(2)}) async-start(bf16[8,17,64,128]{3,2,1,0:T(8,128)(2,1)} %whole_terms.11), calls=%async_computation.3 | async-start | bytes 4456448 | tf_op jit(solution)/shard_map/cond/branch_1_fun/all_to_all | solution.py:535
  56.7 0.0 collective-permute-start.10
  56.7 0.5 collective-permute-start.11
  57.2 6.7 %span_terms.11.refs_6_ = f32[19,64,512]{2,1,0:T(8,128)} custom-call(s32[8]{0:T(128)S(1)} %copy-done.11, f32[2,9]{1,0:T(2,128)S(1)} %copy-done.41, bf16[64,32,512]{2,1,0:T(8,128)(2,1)} %get-tuple-element.281.u_ref, bf16[64,32,512]{2,1,0:T(8,128)(2,1)} %get-tuple-element.299.w_ref), custom_call_target="tpu_custom_call" | custom-call | tf_op jit(solution)/shard_map/cond/branch_1_fun/span_terms/pallas_call | solution.py:217
  63.9 0.6 pad_add_fusion.1.spots_ref
  64.4 0.0 collective-permute-done.10.refs_2_
  64.4 0.0 collective-permute-done.11.refs_3_
  64.5 15.3 %stream_terms.11.base_ref = f32[19,64,512]{2,1,0:T(8,128)} custom-call(s32[4]{0:T(128)} %pad_add_fusion.1.spots_ref, bf16[19,64,512]{2,1,0:T(8,128)(2,1)} %get-tuple-element.283.refs_0_, bf16[19,64,512]{2,1,0:T(8,128)(2,1)} %collective-permute-done.9.refs_1_, bf16[19,64,512]{2,1,0:T(8,128)(2,1)} %collective-permute-done.10.refs_2_, ...), custom_call_target="tpu_custom_call" | custom-call | tf_op jit(solution)/shard_map/cond/branch_1_fun/stream_terms/pallas_call | solution.py:292
  79.8 25.0 %all-to-all-done.3.wall_ref = bf16[8,17,64,128]{3,2,1,0:T(8,128)(2,1)} async-done(((bf16[8,17,64,128]{3,2,1,0:T(8,128)(2,1)}), bf16[8,17,64,128]{3,2,1,0:T(8,128)(2,1)}, u32[]{:S(2)}, u32[]{:S(2)}) %all-to-all-start.3) | async-done | bytes 2228256 | tf_op jit(solution)/shard_map/cond/branch_1_fun/all_to_all | solution.py:535
  104.8 4.9 %finish.11 = bf16[64,32,512]{2,1,0:T(8,128)(2,1)} custom-call(s32[8]{0:T(128)S(1)} %copy-done.11, f32[19,64,512]{2,1,0:T(8,128)} %stream_terms.11.base_ref, bf16[8,17,64,128]{3,2,1,0:T(8,128)(2,1)} %all-to-all-done.3.wall_ref), custom_call_target="tpu_custom_call" | custom-call | tf_op jit(solution)/shard_map/cond/branch_1_fun/finish/pallas_call | solution.py:481
  (7 shorter events, 0.0 us)
Async XLA Ops:
  2.0 11.8 %copy-start.31 = (f32[512]{0:T(512)S(1)}, f32[512]{0:T(512)}, u32[]{:S(2)}) copy-start(f32[512]{0:T(512)} %get-tuple-element.287) | copy-start | bytes 6148 | tf_op jit(solution)/shard_map/cond
  2.1 11.8 %copy-start.1 = (bf16[512,512]{1,0:T(8,128)(2,1)S(1)}, bf16[512,512]{1,0:T(8,128)(2,1)}, u32[]{:S(2)}) copy-start(bf16[512,512]{1,0:T(8,128)(2,1)} %get-tuple-element.288) | copy-start | bytes 1572868 | tf_op jit(solution)/shard_map/cond
  2.1 11.8 %copy-start.21 = (f32[512]{0:T(512)S(1)}, f32[512]{0:T(512)}, u32[]{:S(2)}) copy-start(f32[512]{0:T(512)} %get-tuple-element.289) | copy-start | bytes 6148 | tf_op jit(solution)/shard_map/cond
  7.4 14.5 %collective-permute-start.6 = (bf16[15,2,64,128]{3,2,1,0:T(8,128)(2,1)}, bf16[15,2,64,128]{3,2,1,0:T(8,128)(2,1)}, u32[]{:S(2)}, u32[]{:S(2)}) collective-permute-start(bf16[15,2,64,128]{3,2,1,0:T(8,128)(2,1)} %get-tuple-element.285), channel_id=1, source_target_pairs={{0,1},{1,0},{2,3},{3,2},{4,5},{5,4},{6,7},{7,6},{8,9},{9,8},{10,11... | collective-permute-start | bytes 1474568 | tf_op jit(solution)/shard_map/cond/branch_1_fun/ppermute | solution.py:506
  10.4 17.9 %collective-permute-start.7 = (bf16[15,2,64,128]{3,2,1,0:T(8,128)(2,1)}, bf16[15,2,64,128]{3,2,1,0:T(8,128)(2,1)}, u32[]{:S(2)}, u32[]{:S(2)}) collective-permute-start(bf16[15,2,64,128]{3,2,1,0:T(8,128)(2,1)} %get-tuple-element.293), channel_id=1, source_target_pairs={{0,2},{1,3},{2,0},{3,1},{4,6},{5,7},{6,4},{7,5},{8,10},{9,11},{10,... | collective-permute-start | bytes 1474568 | tf_op jit(solution)/shard_map/cond/branch_1_fun/ppermute | solution.py:506
  11.9 25.1 %collective-permute-start.8 = (bf16[15,2,64,128]{3,2,1,0:T(8,128)(2,1)}, bf16[15,2,64,128]{3,2,1,0:T(8,128)(2,1)}, u32[]{:S(2)}, u32[]{:S(2)}) collective-permute-start(bf16[15,2,64,128]{3,2,1,0:T(8,128)(2,1)} %get-tuple-element.294), channel_id=1, source_target_pairs={{0,3},{1,2},{2,1},{3,0},{4,7},{5,6},{6,5},{7,4},{8,11},{9,10},{10,... | collective-permute-start | bytes 1474568 | tf_op jit(solution)/shard_map/cond/branch_1_fun/ppermute | solution.py:506
  11.9 32.3 %collective-permute-start.9 = (bf16[19,64,512]{2,1,0:T(8,128)(2,1)}, bf16[19,64,512]{2,1,0:T(8,128)(2,1)}, u32[]{:S(2)}, u32[]{:S(2)}) collective-permute-start(bf16[19,64,512]{2,1,0:T(8,128)(2,1)} %get-tuple-element.283.refs_0_), channel_id=1, source_target_pairs={{0,16},{8,24},{16,0},{24,8},{1,17},{9,25},{17,1},{25,9},{2,18},{10... | collective-permute-start | bytes 3735560 | tf_op jit(solution)/shard_map/cond/branch_1_fun/ppermute | solution.py:312
  21.9 22.5 %all-to-all-start.2 = ((bf16[8,2,2,64,128]{4,3,2,1,0:T(8,128)(2,1)}), bf16[8,2,2,64,128]{4,3,2,1,0:T(8,128)(2,1)}, u32[]{:S(2)}, u32[]{:S(2)}) async-start(bf16[8,2,2,64,128]{4,3,2,1,0:T(8,128)(2,1)} %bitcast.9), calls=%async_computation.2 | async-start | bytes 1048576 | tf_op jit(solution)/shard_map/cond/branch_1_fun/all_to_all | solution.py:521
  46.9 10.3 %copy-start.11 = (s32[8]{0:T(128)S(1)}, s32[8]{0:T(128)}, u32[]{:S(2)}) copy-start(s32[8]{0:T(128)} %get-tuple-element.279.counts_ref) | copy-start | bytes 100 | tf_op jit(solution)/shard_map/cond
  46.9 10.3 %copy-start.41 = (f32[2,9]{1,0:T(2,128)S(1)}, f32[2,9]{1,0:T(2,128)}, u32[]{:S(2)}) copy-start(f32[2,9]{1,0:T(2,128)} %get-tuple-element.298.coef_ref) | copy-start | bytes 220 | tf_op jit(solution)/shard_map/cond
  46.9 57.8 %all-to-all-start.3 = ((bf16[8,17,64,128]{3,2,1,0:T(8,128)(2,1)}), bf16[8,17,64,128]{3,2,1,0:T(8,128)(2,1)}, u32[]{:S(2)}, u32[]{:S(2)}) async-start(bf16[8,17,64,128]{3,2,1,0:T(8,128)(2,1)} %whole_terms.11), calls=%async_computation.3 | async-start | bytes 4456448 | tf_op jit(solution)/shard_map/cond/branch_1_fun/all_to_all | solution.py:535
  56.7 7.8 %collective-permute-start.10 = (bf16[19,64,512]{2,1,0:T(8,128)(2,1)}, bf16[19,64,512]{2,1,0:T(8,128)(2,1)}, u32[]{:S(2)}, u32[]{:S(2)}) collective-permute-start(bf16[19,64,512]{2,1,0:T(8,128)(2,1)} %get-tuple-element.283.refs_0_), channel_id=1, source_target_pairs={{0,8},{8,0},{16,24},{24,16},{1,9},{9,1},{17,25},{25,17},{2,10},{10... | collective-permute-start | bytes 3735560 | tf_op jit(solution)/shard_map/cond/branch_1_fun/ppermute | solution.py:312
  56.7 7.8 %collective-permute-start.11 = (bf16[19,64,512]{2,1,0:T(8,128)(2,1)}, bf16[19,64,512]{2,1,0:T(8,128)(2,1)}, u32[]{:S(2)}, u32[]{:S(2)}) collective-permute-start(bf16[19,64,512]{2,1,0:T(8,128)(2,1)} %collective-permute-done.9.refs_1_), channel_id=1, source_target_pairs={{0,8},{8,0},{16,24},{24,16},{1,9},{9,1},{17,25},{25,17},{2,10},{10... | collective-permute-start | bytes 3735560 | tf_op jit(solution)/shard_map/cond/branch_1_fun/ppermute | solution.py:312
